TPU v7x, 512 devices: a whole 4x8x8 slice. The times are simulated.
512 devices in a mesh: blk: 32 (over y, z_hi), team: 16 (over z_lo, x, core).
Axes of the slice: x: 4, y: 8, z: 8 (z_hi: 4, z_lo: 2; z = z_hi * 2 + z_lo), core: 2. Of those that a mesh axis runs over, the one named last changes fastest.
Arguments:
- points: bfloat16 [16, 65536], P(None, ('blk', 'team')), may hold values from -5 to 5
- inv_scale: float32 [16], replicated, may hold values from 0.5 to 1
- noise_var: float32 [65536], P(('blk', 'team')), may hold values from 0.2 to 2
- signal_var: float32 [1], replicated, may hold values from 0.5 to 2
- targets: float32 [32, 65536], P(None, ('blk', 'team')), may hold values from -6 to 6
Outputs:
- solution: float32 [32, 65536], P(None, ('blk', 'team'))
- residual: float32 [32, 65536], P(None, ('blk', 'team'))
All inputs are finite; a program needn't handle non-finite values.
Results may differ from a plain program's by a relative error of at most 0.0048.
Values may be sent and summed in bfloat16 or wider, within the bound.
No kernel may reach another device: no remote copies, remote signals or barrier semaphores. Data moves between devices by JAX's collectives and lax.ppermute only.
A program may use at most 64 MiB of HBM per device.

v0:
```python
import jax
import jax.numpy as jnp
from jax import lax
from jax.sharding import PartitionSpec as P

ITERS = 2


def shards(points, inv_scale, noise_var, signal_var, targets):
    gathered = lax.all_gather(points, ("blk", "team"), axis=1, tiled=True)
    scaled_all = gathered.astype(jnp.float32) * inv_scale[:, None]
    norms_all = jnp.sum(scaled_all * scaled_all, axis=0)
    own_scaled = points.astype(jnp.float32) * inv_scale[:, None]
    own_norms = jnp.sum(own_scaled * own_scaled, axis=0)
    weight = signal_var[0]

    def squares(residual):
        return lax.psum(jnp.sum(residual * residual, axis=1), ("blk", "team"))

    solution = jnp.zeros_like(targets)
    residual = targets
    direction = targets
    norm_now = squares(residual)
    for iteration in range(ITERS):
        lowered = direction.astype(jnp.bfloat16)
        slab = lax.all_gather(lowered, "team", axis=1, tiled=True)
        inner_prod = lax.dot_general(
            own_scaled,
            scaled_all,
            (((0,), (0,)), ((), ())),
            precision=lax.Precision.HIGHEST,
            preferred_element_type=jnp.float32,
        )
        distance = own_norms[:, None] + norms_all[None, :] - 2.0 * inner_prod
        kernel_tile = jnp.exp(-0.5 * distance).astype(jnp.bfloat16)
        total = lax.dot_general(
            lax.all_gather(slab, "blk", axis=1, tiled=True),
            kernel_tile,
            (((1,), (1,)), ((), ())),
            preferred_element_type=jnp.float32,
        )
        applied = noise_var[None, :] * direction + weight * total
        curvature = lax.psum(jnp.sum(direction * applied, axis=1), ("blk", "team"))
        step_size = norm_now / curvature
        solution = solution + step_size[:, None] * direction
        residual = residual - step_size[:, None] * applied
        if iteration + 1 < ITERS:
            norm_next = squares(residual)
            direction = residual + (norm_next / norm_now)[:, None] * direction
            norm_now = norm_next
    return (solution, residual)


def solution(mesh):
    return jax.shard_map(
        shards,
        mesh=mesh,
        in_specs=(P(None, ("blk", "team")), P(), P(("blk", "team")), P(), P(None, ("blk", "team"))),
        out_specs=(P(None, ("blk", "team")), P(None, ("blk", "team"))),
        check_vma=False,
    )
```

profile of v0, /device:TPU:1, one launch (start us, length us, event | category | flops | bytes accessed | tf_op | source)
XLA Modules:
  0.0 670.9 jit_solution(61854665916168831)
XLA Ops:
  7.2 0.0 all-gather.4.cloned.1.call-start
  7.2 0.7 all-gather.4.cloned.1.call-update
  7.9 0.0 all-gather.6.cloned.1.call-start
  7.9 0.7 convert_element_type.19
  8.7 24.4 %all_gather.16 = bf16[32,2048]{1,0:T(8,128)(2,1)} all-gather(bf16[32,128]{1,0:T(8,128)(2,1)S(1)} %convert_element_type.19), channel_id=1, replica_groups=mesh['blk'=32,'team'=16] {'team'}, dimensions={1}, use_global_device_ids=true | all-gather | bytes 139264 | tf_op jit(solution)/shard_map/all_gather | solution.py:26
  33.1 0.0 all-gather.6.cloned.1.call-update
  33.1 0.0 all-gather.8.cloned.1.call-start
  33.8 0.8 multiply_reduce_fusion.5
  34.6 97.2 %all-gather.4.cloned.1.call-done = bf16[16,65536]{1,0:T(8,128)(2,1)} async-done(((bf16[16,128]{1,0:T(8,128)(2,1)}), bf16[16,65536]{1,0:T(8,128)(2,1)}) %all-gather.4.cloned.1.call-update) | async-done | bytes 2097168 | tf_op jit(solution)/shard_map/all_gather | solution.py:10
  131.8 2.7 multiply_reduce_fusion
  134.5 0.0 copy-start
  134.5 0.0 copy-start.1
  134.5 36.1 %fusion.3 = bf16[128,65536]{1,0:T(8,128)(2,1)} fusion(f32[65536]{0:T(1024)S(1)} %multiply_reduce_fusion, f32[128]{0:T(128)S(1)} %multiply_reduce_fusion.5, bf16[16,65536]{1,0:T(8,128)(2,1)} %all-gather.4.cloned.1.call-done, f32[16]{0:T(128)} %param.6, bf16[16,128]{1,0:T(8,128)(2,1)} %param.5), kind=kOutput, calls=%fused_computation.4 | convolution fusion | flops 1654657024 | bytes 19141184 | tf_op jit(solution)/shard_map/dot_general | solution.py:27
  170.6 64.7 %all-gather.6.cloned.1.call-done = bf16[32,65536]{1,0:T(8,128)(2,1)} async-done(((bf16[32,2048]{1,0:T(8,128)(2,1)}), bf16[32,65536]{1,0:T(8,128)(2,1)}) %all-gather.6.cloned.1.call-update) | async-done | bytes 4194320 | tf_op jit(solution)/shard_map/all_gather | solution.py:37
  235.4 0.0 copy-done
  235.4 0.0 copy-done.1
  235.4 12.9 %multiply_reduce_fusion.3 = (f32[32]{0:T(128)S(1)}, f32[32]{0:T(128)S(1)}, f32[32,128]{1,0:T(8,128)S(1)}) fusion(f32[32,128]{1,0:T(8,128)S(1)} %copy-done, bf16[128,65536]{1,0:T(8,128)(2,1)} %fusion.3, bf16[32,65536]{1,0:T(8,128)(2,1)} %all-gather.6.cloned.1.call-done, f32[]{:T(128)} %bitcast.9, f32[128]{0:T(128)S(1)} %copy-done.1), kind=kOutput, calls=%fused_computation.19 | convolution fusion | flops 536899584 | bytes 21005060 | tf_op jit(solution)/shard_map/dot_general | solution.py:36
  248.2 96.1 %all-reduce = (f32[32]{0:T(128)S(1)}, f32[32]{0:T(128)S(1)}) all-reduce(f32[32]{0:T(128)S(1)} %get-tuple-element.3, f32[32]{0:T(128)S(1)} %get-tuple-element.2), channel_id=1, replica_groups=mesh['blk'=32,'team'=16] {'blk','team'}, use_global_device_ids=true, to_apply=%region_1.0 | all-reduce | flops 64 | bytes 512 | tf_op jit(solution)/shard_map/psum | solution.py:18
  344.3 0.2 multiply_reduce_fusion.2
  344.5 93.6 %psum.30 = f32[32]{0:T(128)S(1)} all-reduce(f32[32]{0:T(128)S(1)} %multiply_reduce_fusion.2), channel_id=1, replica_groups=mesh['blk'=32,'team'=16] {'blk','team'}, use_global_device_ids=true, to_apply=%region_7.0 | all-reduce | flops 32 | bytes 256 | tf_op jit(solution)/shard_map/psum | solution.py:18
  438.1 0.1 fusion.9
  438.2 20.9 %all_gather.18 = bf16[32,2048]{1,0:T(8,128)(2,1)} all-gather(bf16[32,128]{1,0:T(8,128)(2,1)S(1)} %get-tuple-element.6), channel_id=1, replica_groups=mesh['blk'=32,'team'=16] {'team'}, dimensions={1}, use_global_device_ids=true | all-gather | bytes 139264 | tf_op jit(solution)/shard_map/all_gather | solution.py:26
  459.0 0.0 all-gather.8.cloned.1.call-update
  459.0 95.6 %all-gather.8.cloned.1.call-done = bf16[32,65536]{1,0:T(8,128)(2,1)} async-done(((bf16[32,2048]{1,0:T(8,128)(2,1)}), bf16[32,65536]{1,0:T(8,128)(2,1)}) %all-gather.8.cloned.1.call-update) | async-done | bytes 4194320 | tf_op jit(solution)/shard_map/all_gather | solution.py:37
  554.6 13.0 %multiply_reduce_fusion.1 = (f32[32]{0:T(128)S(1)}, f32[32,128]{1,0:T(8,128)S(1)}) fusion(f32[32,128]{1,0:T(8,128)S(1)} %get-tuple-element.7, bf16[32,65536]{1,0:T(8,128)(2,1)} %all-gather.8.cloned.1.call-done, bf16[128,65536]{1,0:T(8,128)(2,1)} %fusion.3, f32[]{:T(128)} %bitcast.10, f32[128]{0:T(128)S(1)} %copy-done.1), kind=kOutput, calls=%fused_computation.15 | convolution fusion | flops 536891392 | bytes 21004932 | tf_op jit(solution)/shard_map/dot_general | solution.py:36
  567.6 96.1 %psum.31 = f32[32]{0:T(128)S(1)} all-reduce(f32[32]{0:T(128)S(1)} %get-tuple-element.11), channel_id=1, replica_groups=mesh['blk'=32,'team'=16] {'blk','team'}, use_global_device_ids=true, to_apply=%region_9.0 | all-reduce | flops 32 | bytes 256 | tf_op jit(solution)/shard_map/psum | solution.py:43
  663.7 0.7 multiply_subtract_fusion
  (3 shorter events, 0.0 us)
Async XLA Ops:
  7.2 124.6 %all-gather.4.cloned.1.call-start = ((), (), s32[]{:S(2)}) async-start(), calls=%async_computation | async-start | bytes 2101248 | tf_op jit(solution)/shard_map/all_gather | solution.py:10
  7.9 227.5 %all-gather.6.cloned.1.call-start = ((), (), s32[]{:S(2)}) async-start(), calls=%async_computation.1 | async-start | bytes 4325376 | tf_op jit(solution)/shard_map/all_gather | solution.py:37
  33.1 521.5 %all-gather.8.cloned.1.call-start = ((), (), s32[]{:S(2)}) async-start(), calls=%async_computation.2 | async-start | bytes 4325376 | tf_op jit(solution)/shard_map/all_gather | solution.py:37
  134.5 100.9 %copy-start = (f32[32,128]{1,0:T(8,128)S(1)}, f32[32,128]{1,0:T(8,128)}, u32[]{:S(2)}) copy-start(f32[32,128]{1,0:T(8,128)} %param.9) | copy-start | bytes 49156
  134.5 100.9 %copy-start.1 = (f32[128]{0:T(128)S(1)}, f32[128]{0:T(128)}, u32[]{:S(2)}) copy-start(f32[128]{0:T(128)} %param.7) | copy-start | bytes 1540
Sparse Core Ops, SparseCore 0:
  12.2 119.5 all-gather.3
  135.0 100.3 all-gather.5
  459.2 95.4 all-gather.7
where the time goes:
time: 671 us
  blocking collectives  331 us (49%)
  waiting for transfers between devices  258 us (38%)
  matrix products  62 us (9%)
  between operations  14.4 us (2%)
    psum x2, blocking collectives, squares(): return lax.psum(jnp.sum(residual * residual, axis=1), ('blk', 'team'))  190 us
    all_gather x2, waiting for transfers between devices, shards(): lax.all_gather(slab, 'blk', axis=1, tiled=True)  160 us
    all_gather x1, waiting for transfers between devices, shards(): gathered = lax.all_gather(points, ('blk', 'team'), axis=1, tiled=True)  97.2 us
    psum x1, blocking collectives, shards(): curvature = lax.psum(jnp.sum(direction * applied, axis=1), ('blk', 'team'))  96.1 us
    all_gather x2, blocking collectives, shards(): slab = lax.all_gather(lowered, 'team', axis=1, tiled=True)  45.3 us
    dot_general x1, matrix products, shards(): lax.dot_general(own_scaled, scaled_all, (((0,), (0,)), ((), ())), precisi...  36.1 us
    dot_general x2, matrix products, shards(): lax.dot_general(lax.all_gather(slab, 'blk', axis=1, tiled=True), kernel_t...  25.8 us
  transfers between devices with their start and end apart: 3, of which 3 were waited for; matrix products, arithmetic and copies ran while one was open for 6% of the time, Pallas kernels for 0%

commit v1 on v0

v1 whole, which is shorter than its diff:
```python
import math

import jax
import jax.numpy as jnp
from jax import lax
from jax.experimental import pallas as pl
from jax.experimental.pallas import tpu as pltpu
from jax.sharding import PartitionSpec as P

f32, bf16 = jnp.float32, jnp.bfloat16
DIMS, PROBES, LANES = 16, 32, 128
FEATURES = 128
LOG2E = math.log2(math.e)
VMEM = pl.BlockSpec(memory_space=pltpu.VMEM)
PARAMS = pltpu.CompilerParams(vmem_limit_bytes=24 * 2**20)


def pieces(x):
    hi = x.astype(bf16).astype(f32)
    rest = x - hi
    mid = rest.astype(bf16).astype(f32)
    low = (rest - mid).astype(bf16).astype(f32)
    return hi, mid, low


def features(parts, halves):
    row = lax.broadcasted_iota(jnp.int32, (DIMS, LANES), 0)
    extra = jnp.zeros((DIMS, LANES), f32)
    for place, values in enumerate(halves):
        extra = jnp.where(row == place, jnp.broadcast_to(values, extra.shape), extra)
    blank = jnp.zeros((FEATURES - 4 * DIMS, LANES), f32)
    return jnp.concatenate([*parts, extra, blank], axis=0)


def half_norms(points, inv_scale):
    scaled = points * inv_scale
    return pieces((-0.5 * LOG2E) * jnp.sum(scaled * scaled, axis=0, keepdims=True))


def tile_kernel(inv_scale_ref, cols_ref, rows_ref, tile_ref, partial_ref, lhs, rhs, *, wide, deep):
    inv_scale = inv_scale_ref[...]
    n_cols, n_rows = cols_ref.shape[0], rows_ref.shape[0]
    one = jnp.ones((1, LANES), f32)

    def row_features(i, carry):
        points = rows_ref[i, :DIMS, :].astype(f32)
        weighted = points * (inv_scale * inv_scale * LOG2E)
        block = features(pieces(weighted), (one, one, one, *half_norms(points, inv_scale)))
        lhs[pl.ds(pl.multiple_of(i * LANES, LANES), LANES), :] = block.T.astype(bf16)
        return carry

    def col_features(i, carry):
        points = cols_ref[i].astype(f32)
        block = features((points, points, points), (*half_norms(points, inv_scale), one, one, one))
        rhs[:, pl.ds(pl.multiple_of(i * LANES, LANES), LANES)] = block.astype(bf16)
        return carry

    lax.fori_loop(0, n_rows, row_features, 0, unroll=4)
    lax.fori_loop(0, n_cols, col_features, 0, unroll=4)
    for c in range(0, n_cols * LANES, wide):

        def step(j, total):
            here = pl.ds(pl.multiple_of(j * deep, deep), deep)
            exponent = jnp.dot(lhs[here, :], rhs[:, c : c + wide], preferred_element_type=f32)
            block = jnp.exp2(exponent).astype(bf16)
            tile_ref[here, c : c + wide] = block
            v = jnp.concatenate([rows_ref[j * (deep // LANES) + m, DIMS:, :] for m in range(deep // LANES)], axis=1)
            return total + jnp.dot(v, block, preferred_element_type=f32)

        total = lax.fori_loop(0, n_rows * LANES // deep, step, jnp.zeros((PROBES, wide), f32))
        for m in range(wide // LANES):
            partial_ref[c // LANES + m] = total[:, m * LANES : (m + 1) * LANES]


def apply_kernel(tile_ref, v_ref, partial_ref, *, wide):
    v = jnp.concatenate([v_ref[m] for m in range(v_ref.shape[0])], axis=1)
    for c in range(0, tile_ref.shape[1], wide):
        total = jnp.dot(v, tile_ref[:, c : c + wide], preferred_element_type=f32)
        for m in range(wide // LANES):
            partial_ref[c // LANES + m] = total[:, m * LANES : (m + 1) * LANES]


def shards(points, inv_scale, noise_var, signal_var, targets):
    blks, teams = lax.axis_size("blk"), lax.axis_size("team")
    weight = signal_var[0]

    def to_all(x, axis, size):
        return lax.all_to_all(jnp.broadcast_to(x[None], (size, *x.shape)), axis, 0, 0)

    cols = to_all(points, "team", teams)
    rows = to_all(jnp.concatenate([points, targets.astype(bf16)], axis=0), "blk", blks)
    tile_shape = (blks * LANES, teams * LANES)
    tile, partial = pl.pallas_call(
        lambda *refs: tile_kernel(*refs, wide=1024, deep=1024),
        out_shape=(pltpu.VMEM(tile_shape, bf16), jax.ShapeDtypeStruct((teams, PROBES, LANES), f32)),
        in_specs=[VMEM] * 3,
        out_specs=[VMEM] * 2,
        scratch_shapes=[pltpu.VMEM((tile_shape[0], FEATURES), bf16), pltpu.VMEM((FEATURES, tile_shape[1]), bf16)],
        compiler_params=PARAMS,
        name="tile",
    )(jnp.broadcast_to(inv_scale[:, None], (DIMS, LANES)), cols, rows)

    def operator(field, partial):
        total = jnp.sum(lax.all_to_all(partial, "team", 0, 0), axis=0)
        return noise_var[None, :] * field + weight * total

    applied = operator(targets, partial)
    partial = pl.pallas_call(
        lambda *refs: apply_kernel(*refs, wide=512),
        out_shape=jax.ShapeDtypeStruct((teams, PROBES, LANES), f32),
        in_specs=[VMEM] * 2,
        out_specs=VMEM,
        compiler_params=PARAMS,
        name="apply",
    )(tile, to_all(applied.astype(bf16), "blk", blks))
    twice = operator(applied, partial)

    sums = jnp.stack(
        [
            jnp.sum(a * b, axis=1)
            for a, b in [
                (targets, targets),
                (targets, applied),
                (applied, applied),
                (targets, twice),
                (applied, twice),
            ]
        ]
    )
    sums = jnp.sum(to_all(sums, "team", teams), axis=0)
    sums = jnp.sum(to_all(sums, "blk", blks), axis=0)
    tt, ta, aa, tb, ab = [sums[i][:, None] for i in range(5)]
    step_0 = tt / ta
    norm_1 = tt - 2.0 * step_0 * ta + step_0 * step_0 * aa
    ratio = norm_1 / tt
    curvature = (1 + ratio) * (1 + ratio) * ta - (1 + ratio) * step_0 * (tb + aa) + step_0 * step_0 * ab
    step_1 = norm_1 / curvature
    residual = targets - step_0 * applied
    direction = residual + ratio * targets
    field = (1 + ratio) * applied - step_0 * twice
    return step_0 * targets + step_1 * direction, residual - step_1 * field


def solution(mesh):
    return jax.shard_map(
        shards,
        mesh=mesh,
        in_specs=(P(None, ("blk", "team")), P(), P(("blk", "team")), P(), P(None, ("blk", "team"))),
        out_specs=(P(None, ("blk", "team")), P(None, ("blk", "team"))),
        check_vma=False,
    )
```

time: 671 us -> 142 us (0.21)
  blocking collectives: 331 us -> 81 us
  waiting for transfers between devices: 258 us -> 11.1 us
  matrix products: 62 us -> 0 us
  starting transfers between devices: 0.12 us -> 15.9 us
  local copies, waits for them, and re-layouts: 0.01 us -> 14.5 us
  between operations: 14.4 us -> 1.39 us
  Pallas kernels: 0 us -> 13 us
    psum x3 -> x0, blocking collectives: 286 us -> none  [the longest x2 190 us: squares(): return lax.psum(jnp.sum(residual * residual, axis=1), ('blk', 'team'))]
    all_gather x3 -> x0, waiting for transfers between devices: 258 us -> none  [the longest x2 160 us: shards(): lax.all_gather(slab, 'blk', axis=1, tiled=True)]
    all_to_all x0 -> x5, blocking collectives: none -> 81 us  [the longest x4 67.8 us: to_all(): lax.all_to_all(jnp.broadcast_to(x[None], (size, *x.shape)), axis, 0, 0)]
    dot_general x3 -> x0, matrix products: 62 us -> none  [the longest x1 36.1 us: shards(): lax.dot_general(own_scaled, scaled_all, (((0,), (0,)), ((), ())), precisi...]
    all_gather x2 -> x0, blocking collectives: 45.3 us -> none  [shards(): slab = lax.all_gather(lowered, 'team', axis=1, tiled=True)]
    all_to_all x0 -> x2, starting transfers between devices: none -> 15.9 us  [the longest x1 10.2 us: to_all(): lax.all_to_all(jnp.broadcast_to(x[None], (size, *x.shape)), axis, 0, 0)]
    pallas_call x0 -> x2, Pallas kernels: none -> 13 us  [the longest x1 10 us: shards(): pl.pallas_call(lambda *refs: tile_kernel(*refs, wide=1024, deep=1024), ou...]
    unnamed x4 -> x12, local copies, waits for them, and re-layouts: 0.01 us -> 11.8 us
  transfers between devices with their start and end apart: 3 -> 2, of which waited for: 3 -> 2; matrix products, arithmetic and copies ran while one was open for 6% -> 1% of each run, Pallas kernels for 0% -> 0%
where the time goes in v1:
time: 142 us; the launch traced here: 141 us
  blocking collectives  81 us (57%)
  starting transfers between devices  15.9 us (11%)
  local copies, waits for them, and re-layouts  14.5 us (10%)
  Pallas kernels  13 us (9%)
  waiting for transfers between devices  11.1 us (8%)
  other arithmetic  4.57 us (3%)
    all_to_all x4, blocking collectives, to_all(): lax.all_to_all(jnp.broadcast_to(x[None], (size, *x.shape)), axis, 0, 0)  67.8 us
    all_to_all x1, blocking collectives, operator(): total = jnp.sum(lax.all_to_all(partial, 'team', 0, 0), axis=0)  13.2 us
    unnamed x12, local copies, waits for them, and re-layouts  11.8 us
    all_to_all x1, starting transfers between devices, to_all(): lax.all_to_all(jnp.broadcast_to(x[None], (size, *x.shape)), axis, 0, 0)  10.2 us
    pallas_call x1, Pallas kernels, shards(): pl.pallas_call(lambda *refs: tile_kernel(*refs, wide=1024, deep=1024), ou...  10 us
    all_to_all x1, waiting for transfers between devices, operator(): total = jnp.sum(lax.all_to_all(partial, 'team', 0, 0), axis=0)  6.59 us
    all_to_all x1, starting transfers between devices, operator(): total = jnp.sum(lax.all_to_all(partial, 'team', 0, 0), axis=0)  5.78 us
    all_to_all x1, waiting for transfers between devices, to_all(): lax.all_to_all(jnp.broadcast_to(x[None], (size, *x.shape)), axis, 0, 0)  4.48 us
  transfers between devices with their start and end apart: 2, of which 2 were waited for; matrix products, arithmetic and copies ran while one was open for 1% of the time, Pallas kernels for 0%

profile of v1, /device:TPU:1, one launch (start us, length us, event | category | flops | bytes accessed | tf_op | source)
XLA Modules:
  0.0 141.5 jit_solution(517760697863448137)
XLA Ops:
  0.6 0.0 copy-start.2
  0.6 0.0 copy-start.3
  0.7 1.3 broadcast_in_dim.13
  2.0 10.2 %all-to-all-start = ((bf16[16,16,128]{2,1,0:T(8,128)(2,1)}), bf16[16,16,128]{2,1,0:T(8,128)(2,1)S(1)}, u32[]{:S(2)}, u32[]{:S(2)}) async-start(bf16[16,16,128]{2,1,0:T(8,128)(2,1)} %broadcast_in_dim.13), calls=%async_computation | async-start | bytes 131072 | tf_op jit(solution)/shard_map/all_to_all | solution.py:88
  12.1 0.7 convert_element_type.6
  12.9 0.7 pad_maximum_fusion
  13.5 4.5 %all-to-all-done.refs_1_ = bf16[16,16,128]{2,1,0:T(8,128)(2,1)S(1)} async-done(((bf16[16,16,128]{2,1,0:T(8,128)(2,1)}), bf16[16,16,128]{2,1,0:T(8,128)(2,1)S(1)}, u32[]{:S(2)}, u32[]{:S(2)}) %all-to-all-start) | async-done | bytes 65568 | tf_op jit(solution)/shard_map/all_to_all | solution.py:88
  18.0 0.1 broadcast_in_dim.14
  18.1 26.7 %all_to_all.35.refs_2_ = bf16[32,48,128]{2,1,0:T(8,128)(2,1)S(1)} all-to-all(bf16[32,48,128]{2,1,0:T(8,128)(2,1)S(1)} %broadcast_in_dim.14), channel_id=1, replica_groups=mesh['blk'=32,'team'=16] {'blk'}, dimensions={0} | all-to-all | bytes 786432 | tf_op jit(solution)/shard_map/all_to_all | solution.py:88
  44.8 0.7 broadcast_in_dim.12.refs_0_
  45.5 10.0 %tile.1 = (bf16[4096,2048]{1,0:T(8,128)(2,1)S(1)}, f32[16,32,128]{2,1,0:T(8,128)}) custom-call(f32[16,128]{1,0:T(8,128)S(1)} %broadcast_in_dim.12.refs_0_, bf16[16,16,128]{2,1,0:T(8,128)(2,1)S(1)} %all-to-all-done.refs_1_, bf16[32,48,128]{2,1,0:T(8,128)(2,1)S(1)} %all_to_all.35.refs_2_), custom_call_target="tpu_custom_call" | custom-call | tf_op jit(solution)/shard_map/tile/pallas_call | solution.py:93
  55.5 0.0 copy-start
  55.5 5.7 %copy-done = bf16[4096,2048]{1,0:T(8,128)(2,1)} copy-done((bf16[4096,2048]{1,0:T(8,128)(2,1)}, bf16[4096,2048]{1,0:T(8,128)(2,1)S(1)}, u32[]{:S(2)}) %copy-start) | copy-done | bytes 16777240
  61.2 5.8 %all-to-all-start.2 = ((f32[16,32,128]{2,1,0:T(8,128)}), f32[16,32,128]{2,1,0:T(8,128)S(1)}, u32[]{:S(2)}, u32[]{:S(2)}) async-start(f32[16,32,128]{2,1,0:T(8,128)} %get-tuple-element.4), calls=%async_computation.2 | async-start | bytes 524288 | tf_op jit(solution)/shard_map/all_to_all | solution.py:104
  67.6 6.6 %all-to-all-done.2 = f32[16,32,128]{2,1,0:T(8,128)S(1)} async-done(((f32[16,32,128]{2,1,0:T(8,128)}), f32[16,32,128]{2,1,0:T(8,128)S(1)}, u32[]{:S(2)}, u32[]{:S(2)}) %all-to-all-start.2) | async-done | bytes 262176 | tf_op jit(solution)/shard_map/all_to_all | solution.py:104
  74.3 0.7 fusion.7
  75.0 16.5 %all_to_all.36.refs_1_ = bf16[32,32,128]{2,1,0:T(8,128)(2,1)S(1)} all-to-all(bf16[32,32,128]{2,1,0:T(8,128)(2,1)S(1)} %broadcast_in_dim.15), channel_id=1, replica_groups=mesh['blk'=32,'team'=16] {'blk'}, dimensions={0} | all-to-all | bytes 524288 | tf_op jit(solution)/shard_map/all_to_all | solution.py:88
  91.6 0.0 copy-start.1
  91.6 5.8 %copy-done.1 = bf16[4096,2048]{1,0:T(8,128)(2,1)S(1)} copy-done((bf16[4096,2048]{1,0:T(8,128)(2,1)S(1)}, bf16[4096,2048]{1,0:T(8,128)(2,1)}, u32[]{:S(2)}) %copy-start.1) | copy-done | bytes 16777240
  97.3 2.9 %apply.1 = f32[16,32,128]{2,1,0:T(8,128)S(1)} custom-call(bf16[4096,2048]{1,0:T(8,128)(2,1)S(1)} %copy-done.1, bf16[32,32,128]{2,1,0:T(8,128)(2,1)S(1)} %all_to_all.36.refs_1_), custom_call_target="tpu_custom_call" | custom-call | tf_op jit(solution)/shard_map/apply/pallas_call | solution.py:108
  100.3 13.2 %all_to_all.37 = f32[16,32,128]{2,1,0:T(8,128)S(1)} all-to-all(f32[16,32,128]{2,1,0:T(8,128)S(1)} %apply.1), channel_id=1, replica_groups=mesh['blk'=32,'team'=16] {'team'}, dimensions={0} | all-to-all | bytes 524288 | tf_op jit(solution)/shard_map/all_to_all | solution.py:104
  113.5 0.0 copy-done.2
  113.5 0.0 copy-done.3
  113.5 0.2 multiply_reduce_fusion
  113.8 0.1 reshape.139
  113.9 9.2 %all_to_all.38 = f32[16,1,160]{2,1,0:T(1,128)S(1)} all-to-all(f32[16,1,160]{2,1,0:T(1,128)S(1)} %reshape.139), channel_id=1, replica_groups=mesh['blk'=32,'team'=16] {'team'}, dimensions={0} | all-to-all | bytes 20480 | tf_op jit(solution)/shard_map/all_to_all | solution.py:88
  123.1 0.5 broadcast.33
  123.6 0.7 reduce
  124.3 0.1 reshape.140
  124.4 0.1 reshape.141
  124.5 15.4 %all_to_all.39 = f32[32,1,160]{2,1,0:T(1,128)S(1)} all-to-all(f32[32,1,160]{2,1,0:T(1,128)S(1)} %reshape.141), channel_id=1, replica_groups=mesh['blk'=32,'team'=16] {'blk'}, dimensions={0} | all-to-all | bytes 40960 | tf_op jit(solution)/shard_map/all_to_all | solution.py:88
  139.9 0.7 reduce.1
  140.6 0.1 reshape.142
  140.8 0.7 multiply_subtract_fusion
  (10 shorter events, 0.2 us)
Async XLA Ops:
  0.6 112.9 %copy-start.2 = (f32[32,128]{1,0:T(8,128)S(1)}, f32[32,128]{1,0:T(8,128)}, u32[]{:S(2)}) copy-start(f32[32,128]{1,0:T(8,128)} %param.9) | copy-start | bytes 49156
  0.6 112.9 %copy-start.3 = (f32[128]{0:T(128)S(1)}, f32[128]{0:T(128)}, u32[]{:S(2)}) copy-start(f32[128]{0:T(128)} %param.7) | copy-start | bytes 1540
  2.0 16.1 %all-to-all-start = ((bf16[16,16,128]{2,1,0:T(8,128)(2,1)}), bf16[16,16,128]{2,1,0:T(8,128)(2,1)S(1)}, u32[]{:S(2)}, u32[]{:S(2)}) async-start(bf16[16,16,128]{2,1,0:T(8,128)(2,1)} %broadcast_in_dim.13), calls=%async_computation | async-start | bytes 131072 | tf_op jit(solution)/shard_map/all_to_all | solution.py:88
  55.5 5.7 %copy-start = (bf16[4096,2048]{1,0:T(8,128)(2,1)}, bf16[4096,2048]{1,0:T(8,128)(2,1)S(1)}, u32[]{:S(2)}) copy-start(bf16[4096,2048]{1,0:T(8,128)(2,1)S(1)} %get-tuple-element.5.refs_0_) | copy-start | bytes 50331652
  61.2 13.0 %all-to-all-start.2 = ((f32[16,32,128]{2,1,0:T(8,128)}), f32[16,32,128]{2,1,0:T(8,128)S(1)}, u32[]{:S(2)}, u32[]{:S(2)}) async-start(f32[16,32,128]{2,1,0:T(8,128)} %get-tuple-element.4), calls=%async_computation.2 | async-start | bytes 524288 | tf_op jit(solution)/shard_map/all_to_all | solution.py:104
  91.6 5.8 %copy-start.1 = (bf16[4096,2048]{1,0:T(8,128)(2,1)S(1)}, bf16[4096,2048]{1,0:T(8,128)(2,1)}, u32[]{:S(2)}) copy-start(bf16[4096,2048]{1,0:T(8,128)(2,1)} %copy-done) | copy-start | bytes 50331652

commit v2 on v1

--- a/solution.py
+++ b/solution.py
@@ -87,6 +87,9 @@
     def to_all(x, axis, size):
         return lax.all_to_all(jnp.broadcast_to(x[None], (size, *x.shape)), axis, 0, 0)
 
+    points, inv_scale = lax.optimization_barrier(
+        (points, jnp.broadcast_to(inv_scale[:, None], (DIMS, LANES)))
+    )
     cols = to_all(points, "team", teams)
     rows = to_all(jnp.concatenate([points, targets.astype(bf16)], axis=0), "blk", blks)
     tile_shape = (blks * LANES, teams * LANES)
@@ -98,7 +101,7 @@
         scratch_shapes=[pltpu.VMEM((tile_shape[0], FEATURES), bf16), pltpu.VMEM((FEATURES, tile_shape[1]), bf16)],
         compiler_params=PARAMS,
         name="tile",
-    )(jnp.broadcast_to(inv_scale[:, None], (DIMS, LANES)), cols, rows)
+    )(inv_scale, cols, rows)
 
     def operator(field, partial):
         total = jnp.sum(lax.all_to_all(partial, "team", 0, 0), axis=0)
@@ -112,7 +115,7 @@
         out_specs=VMEM,
         compiler_params=PARAMS,
         name="apply",
-    )(tile, to_all(applied.astype(bf16), "blk", blks))
+    )(pltpu.with_memory_space_constraint(tile, pltpu.VMEM), to_all(applied.astype(bf16), "blk", blks))
     twice = operator(applied, partial)
 
     sums = jnp.stack(

time: 142 us -> 142 us (level)
  no operation moved by 1% of the time
where the time goes in v2:
time: 142 us; the launch traced here: 141 us
  blocking collectives  81 us (57%)
  starting transfers between devices  16 us (11%)
  local copies, waits for them, and re-layouts  14.5 us (10%)
  Pallas kernels  12.9 us (9%)
  waiting for transfers between devices  11.1 us (8%)
  other arithmetic  4.57 us (3%)
    all_to_all x4, blocking collectives, to_all(): lax.all_to_all(jnp.broadcast_to(x[None], (size, *x.shape)), axis, 0, 0)  67.8 us
    all_to_all x1, blocking collectives, operator(): total = jnp.sum(lax.all_to_all(partial, 'team', 0, 0), axis=0)  13.2 us
    unnamed x12, local copies, waits for them, and re-layouts  11.8 us
    all_to_all x1, starting transfers between devices, to_all(): lax.all_to_all(jnp.broadcast_to(x[None], (size, *x.shape)), axis, 0, 0)  10.2 us
    pallas_call x1, Pallas kernels, shards(): pl.pallas_call(lambda *refs: tile_kernel(*refs, wide=1024, deep=1024), ou...  10 us
    all_to_all x1, waiting for transfers between devices, operator(): total = jnp.sum(lax.all_to_all(partial, 'team', 0, 0), axis=0)  6.59 us
    all_to_all x1, starting transfers between devices, operator(): total = jnp.sum(lax.all_to_all(partial, 'team', 0, 0), axis=0)  5.8 us
    all_to_all x1, waiting for transfers between devices, to_all(): lax.all_to_all(jnp.broadcast_to(x[None], (size, *x.shape)), axis, 0, 0)  4.49 us
  transfers between devices with their start and end apart: 2, of which 2 were waited for; matrix products, arithmetic and copies ran while one was open for 1% of the time, Pallas kernels for 0%

profile of v2, /device:TPU:1, one launch (start us, length us, event | category | flops | bytes accessed | tf_op | source)
XLA Modules:
  0.0 141.5 jit_solution(6191324339465131037)
XLA Ops:
  0.6 0.0 copy-start.2
  0.6 0.0 copy-start.3
  0.7 0.7 broadcast_in_dim.12.refs_0_
  1.4 1.3 broadcast_in_dim.13
  2.7 10.2 %all-to-all-start = ((bf16[16,16,128]{2,1,0:T(8,128)(2,1)}), bf16[16,16,128]{2,1,0:T(8,128)(2,1)S(1)}, u32[]{:S(2)}, u32[]{:S(2)}) async-start(bf16[16,16,128]{2,1,0:T(8,128)(2,1)} %broadcast_in_dim.13), calls=%async_computation | async-start | bytes 131072 | tf_op jit(solution)/shard_map/all_to_all | solution.py:88
  12.9 0.7 convert_element_type.6
  13.6 0.7 pad_maximum_fusion
  14.3 4.5 %all-to-all-done.refs_1_ = bf16[16,16,128]{2,1,0:T(8,128)(2,1)S(1)} async-done(((bf16[16,16,128]{2,1,0:T(8,128)(2,1)}), bf16[16,16,128]{2,1,0:T(8,128)(2,1)S(1)}, u32[]{:S(2)}, u32[]{:S(2)}) %all-to-all-start) | async-done | bytes 65568 | tf_op jit(solution)/shard_map/all_to_all | solution.py:88
  18.8 0.1 broadcast_in_dim.14
  18.8 26.7 %all_to_all.35.refs_2_ = bf16[32,48,128]{2,1,0:T(8,128)(2,1)S(1)} all-to-all(bf16[32,48,128]{2,1,0:T(8,128)(2,1)S(1)} %broadcast_in_dim.14), channel_id=1, replica_groups=mesh['blk'=32,'team'=16] {'blk'}, dimensions={0} | all-to-all | bytes 786432 | tf_op jit(solution)/shard_map/all_to_all | solution.py:88
  45.5 10.0 %tile.1 = (bf16[4096,2048]{1,0:T(8,128)(2,1)S(1)}, f32[16,32,128]{2,1,0:T(8,128)}) custom-call(f32[16,128]{1,0:T(8,128)S(1)} %broadcast_in_dim.12.refs_0_, bf16[16,16,128]{2,1,0:T(8,128)(2,1)S(1)} %all-to-all-done.refs_1_, bf16[32,48,128]{2,1,0:T(8,128)(2,1)S(1)} %all_to_all.35.refs_2_), custom_call_target="tpu_custom_call" | custom-call | tf_op jit(solution)/shard_map/tile/pallas_call | solution.py:96
  55.5 0.0 copy-start
  55.5 5.7 %copy-done = bf16[4096,2048]{1,0:T(8,128)(2,1)} copy-done((bf16[4096,2048]{1,0:T(8,128)(2,1)}, bf16[4096,2048]{1,0:T(8,128)(2,1)S(1)}, u32[]{:S(2)}) %copy-start) | copy-done | bytes 16777240
  61.2 5.8 %all-to-all-start.2 = ((f32[16,32,128]{2,1,0:T(8,128)}), f32[16,32,128]{2,1,0:T(8,128)S(1)}, u32[]{:S(2)}, u32[]{:S(2)}) async-start(f32[16,32,128]{2,1,0:T(8,128)} %get-tuple-element.8), calls=%async_computation.2 | async-start | bytes 524288 | tf_op jit(solution)/shard_map/all_to_all | solution.py:107
  67.7 6.6 %all-to-all-done.2 = f32[16,32,128]{2,1,0:T(8,128)S(1)} async-done(((f32[16,32,128]{2,1,0:T(8,128)}), f32[16,32,128]{2,1,0:T(8,128)S(1)}, u32[]{:S(2)}, u32[]{:S(2)}) %all-to-all-start.2) | async-done | bytes 262176 | tf_op jit(solution)/shard_map/all_to_all | solution.py:107
  74.3 0.7 fusion.7
  75.0 16.5 %all_to_all.36.refs_1_ = bf16[32,32,128]{2,1,0:T(8,128)(2,1)S(1)} all-to-all(bf16[32,32,128]{2,1,0:T(8,128)(2,1)S(1)} %broadcast_in_dim.15), channel_id=1, replica_groups=mesh['blk'=32,'team'=16] {'blk'}, dimensions={0} | all-to-all | bytes 524288 | tf_op jit(solution)/shard_map/all_to_all | solution.py:88
  91.6 0.0 copy-start.1
  91.6 5.8 %copy-done.1 = bf16[4096,2048]{1,0:T(8,128)(2,1)S(1)} copy-done((bf16[4096,2048]{1,0:T(8,128)(2,1)S(1)}, bf16[4096,2048]{1,0:T(8,128)(2,1)}, u32[]{:S(2)}) %copy-start.1) | copy-done | bytes 16777240
  97.3 2.9 %apply.1 = f32[16,32,128]{2,1,0:T(8,128)S(1)} custom-call(bf16[4096,2048]{1,0:T(8,128)(2,1)S(1)} %copy-done.1, bf16[32,32,128]{2,1,0:T(8,128)(2,1)S(1)} %all_to_all.36.refs_1_), custom_call_target="tpu_custom_call" | custom-call | tf_op jit(solution)/shard_map/apply/pallas_call | solution.py:111
  100.3 13.2 %all_to_all.37 = f32[16,32,128]{2,1,0:T(8,128)S(1)} all-to-all(f32[16,32,128]{2,1,0:T(8,128)S(1)} %apply.1), channel_id=1, replica_groups=mesh['blk'=32,'team'=16] {'team'}, dimensions={0} | all-to-all | bytes 524288 | tf_op jit(solution)/shard_map/all_to_all | solution.py:107
  113.5 0.0 copy-done.2
  113.5 0.0 copy-done.3
  113.5 0.2 multiply_reduce_fusion
  113.8 0.1 reshape.139
  113.9 9.2 %all_to_all.38 = f32[16,1,160]{2,1,0:T(1,128)S(1)} all-to-all(f32[16,1,160]{2,1,0:T(1,128)S(1)} %reshape.139), channel_id=1, replica_groups=mesh['blk'=32,'team'=16] {'team'}, dimensions={0} | all-to-all | bytes 20480 | tf_op jit(solution)/shard_map/all_to_all | solution.py:88
  123.1 0.5 broadcast.33
  123.6 0.7 reduce
  124.3 0.1 reshape.140
  124.4 0.1 reshape.141
  124.5 15.4 %all_to_all.39 = f32[32,1,160]{2,1,0:T(1,128)S(1)} all-to-all(f32[32,1,160]{2,1,0:T(1,128)S(1)} %reshape.141), channel_id=1, replica_groups=mesh['blk'=32,'team'=16] {'blk'}, dimensions={0} | all-to-all | bytes 40960 | tf_op jit(solution)/shard_map/all_to_all | solution.py:88
  139.9 0.7 reduce.1
  140.6 0.1 reshape.142
  140.8 0.7 multiply_subtract_fusion
  (10 shorter events, 0.2 us)
Async XLA Ops:
  0.6 112.9 %copy-start.2 = (f32[32,128]{1,0:T(8,128)S(1)}, f32[32,128]{1,0:T(8,128)}, u32[]{:S(2)}) copy-start(f32[32,128]{1,0:T(8,128)} %param.9) | copy-start | bytes 49156
  0.6 112.9 %copy-start.3 = (f32[128]{0:T(128)S(1)}, f32[128]{0:T(128)}, u32[]{:S(2)}) copy-start(f32[128]{0:T(128)} %param.7) | copy-start | bytes 1540
  2.7 16.1 %all-to-all-start = ((bf16[16,16,128]{2,1,0:T(8,128)(2,1)}), bf16[16,16,128]{2,1,0:T(8,128)(2,1)S(1)}, u32[]{:S(2)}, u32[]{:S(2)}) async-start(bf16[16,16,128]{2,1,0:T(8,128)(2,1)} %broadcast_in_dim.13), calls=%async_computation | async-start | bytes 131072 | tf_op jit(solution)/shard_map/all_to_all | solution.py:88
  55.5 5.7 %copy-start = (bf16[4096,2048]{1,0:T(8,128)(2,1)}, bf16[4096,2048]{1,0:T(8,128)(2,1)S(1)}, u32[]{:S(2)}) copy-start(bf16[4096,2048]{1,0:T(8,128)(2,1)S(1)} %get-tuple-element.9.refs_0_) | copy-start | bytes 50331652
  61.2 13.0 %all-to-all-start.2 = ((f32[16,32,128]{2,1,0:T(8,128)}), f32[16,32,128]{2,1,0:T(8,128)S(1)}, u32[]{:S(2)}, u32[]{:S(2)}) async-start(f32[16,32,128]{2,1,0:T(8,128)} %get-tuple-element.8), calls=%async_computation.2 | async-start | bytes 524288 | tf_op jit(solution)/shard_map/all_to_all | solution.py:107
  91.6 5.8 %copy-start.1 = (bf16[4096,2048]{1,0:T(8,128)(2,1)S(1)}, bf16[4096,2048]{1,0:T(8,128)(2,1)}, u32[]{:S(2)}) copy-start(bf16[4096,2048]{1,0:T(8,128)(2,1)} %copy-done) | copy-start | bytes 50331652

commit v3 on v2

v3 whole, which is shorter than its diff:
```python
import math

import jax
import jax.numpy as jnp
from jax import lax
from jax.experimental import pallas as pl
from jax.experimental.pallas import tpu as pltpu
from jax.sharding import PartitionSpec as P

f32, bf16 = jnp.float32, jnp.bfloat16
DIMS, PROBES, LANES = 16, 32, 128
FEATURES = 128
EXTRA = 8
LOG2E = math.log2(math.e)
VMEM = pl.BlockSpec(memory_space=pltpu.VMEM)
HBM = pl.BlockSpec(memory_space=pltpu.HBM)
LARGE = pltpu.CompilerParams(vmem_limit_bytes=24 * 2**20)
SMALL = pltpu.CompilerParams(vmem_limit_bytes=8 * 2**20)


def pieces(x):
    hi = x.astype(bf16).astype(f32)
    rest = x - hi
    mid = rest.astype(bf16).astype(f32)
    low = (rest - mid).astype(bf16).astype(f32)
    return hi, mid, low


def features(parts, halves):
    row = lax.broadcasted_iota(jnp.int32, (DIMS, LANES), 0)
    extra = jnp.zeros((DIMS, LANES), f32)
    for place, values in enumerate(halves):
        extra = jnp.where(row == place, jnp.broadcast_to(values, extra.shape), extra)
    blank = jnp.zeros((FEATURES - 4 * DIMS, LANES), f32)
    return jnp.concatenate([*parts, extra, blank], axis=0)


def half_norms(points, inv_scale):
    scaled = points * inv_scale
    return pieces((-0.5 * LOG2E) * jnp.sum(scaled * scaled, axis=0, keepdims=True))


def tile_kernel(inv_scale_ref, cols_ref, rows_ref, tile_ref, partial_ref, lhs, rhs, held, sems, *, deep):
    inv_scale = inv_scale_ref[...]
    n_cols, n_rows = cols_ref.shape[0], rows_ref.shape[0]
    one = jnp.ones((1, LANES), f32)

    def row_features(i, carry):
        points = rows_ref[i, :DIMS, :].astype(f32)
        weighted = points * (inv_scale * inv_scale * LOG2E)
        block = features(pieces(weighted), (one, one, one, *half_norms(points, inv_scale)))
        lhs[pl.ds(pl.multiple_of(i * LANES, LANES), LANES), :] = block.T.astype(bf16)
        return carry

    def col_features(i, carry):
        points = cols_ref[i].astype(f32)
        block = features((points, points, points), (*half_norms(points, inv_scale), one, one, one))
        rhs[:, pl.ds(pl.multiple_of(i * LANES, LANES), LANES)] = block.astype(bf16)
        return carry

    lax.fori_loop(0, n_rows, row_features, 0, unroll=4)
    lax.fori_loop(0, n_cols, col_features, 0, unroll=4)

    def copy(j):
        here = pl.ds(pl.multiple_of(j * deep, deep), deep)
        return pltpu.make_async_copy(held.at[here, :], tile_ref.at[here, :], sems.at[j])

    chunks = n_rows * LANES // deep

    def step(j, total):
        here = pl.ds(pl.multiple_of(j * deep, deep), deep)
        exponent = jnp.dot(lhs[here, :], rhs[...], preferred_element_type=f32)
        block = jnp.exp2(exponent).astype(bf16)
        held[here, :] = block
        copy(j).start()
        v = jnp.concatenate([rows_ref[j * (deep // LANES) + m, DIMS:, :] for m in range(deep // LANES)], axis=1)
        return total + jnp.dot(v, block, preferred_element_type=f32)

    total = lax.fori_loop(0, chunks, step, jnp.zeros((PROBES, n_cols * LANES), f32))
    for m in range(n_cols):
        partial_ref[m] = total[:, m * LANES : (m + 1) * LANES]
    for j in range(chunks):
        copy(j).wait()


def apply_kernel(tile_ref, v_ref, partial_ref, held, sems, *, deep):
    chunks = tile_ref.shape[0] // deep

    def copy(j):
        here = pl.ds(pl.multiple_of(j * deep, deep), deep)
        return pltpu.make_async_copy(tile_ref.at[here, :], held.at[here, :], sems.at[j])

    for j in range(chunks):
        copy(j).start()

    def step(j, total):
        here = pl.ds(pl.multiple_of(j * deep, deep), deep)
        copy(j).wait()
        v = jnp.concatenate([v_ref[j * (deep // LANES) + m] for m in range(deep // LANES)], axis=1)
        return total + jnp.dot(v, held[here, :], preferred_element_type=f32)

    total = lax.fori_loop(0, chunks, step, jnp.zeros((PROBES, tile_ref.shape[1]), f32))
    for m in range(partial_ref.shape[0]):
        partial_ref[m] = total[:, m * LANES : (m + 1) * LANES]


def pack_kernel(weight_ref, partial_ref, cols_ref, targets_ref, applied_ref, noise_ref, message_ref):
    targets, applied = targets_ref[...], applied_ref[...]
    inner = jnp.zeros(targets.shape, f32)
    for m in range(partial_ref.shape[0]):
        message_ref[m, :PROBES, :] = partial_ref[m]
        inner = inner + cols_ref[m].astype(f32) * partial_ref[m]
    inner = weight_ref[0] * inner + noise_ref[...] * applied * applied
    lane = lax.broadcasted_iota(jnp.int32, (PROBES, LANES), 1)
    sums = jnp.zeros((PROBES, LANES), f32)
    for place, product in enumerate((targets * targets, targets * applied, applied * applied, inner)):
        sums = jnp.where(lane == place, jnp.sum(product, axis=1, keepdims=True), sums)
    sums = jnp.concatenate([sums, jnp.zeros((LANES - PROBES, LANES), f32)], axis=0).T[:EXTRA]
    for m in range(partial_ref.shape[0]):
        message_ref[m, PROBES:, :] = sums


def shards(points, inv_scale, noise_var, signal_var, targets):
    blks, teams = lax.axis_size("blk"), lax.axis_size("team")
    weight = signal_var[0]

    def to_all(x, axis, size):
        return lax.all_to_all(jnp.broadcast_to(x[None], (size, *x.shape)), axis, 0, 0)

    points, inv_scale = lax.optimization_barrier(
        (points, jnp.broadcast_to(inv_scale[:, None], (DIMS, LANES)))
    )
    cols = to_all(points, "team", teams)
    rows = to_all(jnp.concatenate([points, targets.astype(bf16)], axis=0), "blk", blks)
    tile_shape = (blks * LANES, teams * LANES)
    deep = 512
    sems = pltpu.SemaphoreType.DMA((tile_shape[0] // deep,))
    tile, partial = pl.pallas_call(
        lambda *refs: tile_kernel(*refs, deep=deep),
        out_shape=(pltpu.HBM(tile_shape, bf16), jax.ShapeDtypeStruct((teams, PROBES, LANES), f32)),
        in_specs=[VMEM] * 3,
        out_specs=[HBM, VMEM],
        scratch_shapes=[
            pltpu.VMEM((tile_shape[0], FEATURES), bf16),
            pltpu.VMEM((FEATURES, tile_shape[1]), bf16),
            pltpu.VMEM(tile_shape, bf16),
            sems,
        ],
        compiler_params=LARGE,
        name="tile",
    )(inv_scale, cols, rows)

    total = jnp.sum(lax.all_to_all(partial, "team", 0, 0), axis=0)
    applied = noise_var[None, :] * targets + weight * total
    lowered = applied.astype(bf16)
    partial = pl.pallas_call(
        lambda *refs: apply_kernel(*refs, deep=deep),
        out_shape=jax.ShapeDtypeStruct((teams, PROBES, LANES), f32),
        in_specs=[HBM, VMEM],
        out_specs=VMEM,
        scratch_shapes=[pltpu.VMEM(tile_shape, bf16), sems],
        compiler_params=LARGE,
        cost_estimate=pl.CostEstimate(
            flops=2 * PROBES * tile_shape[0] * tile_shape[1],
            bytes_accessed=2 * tile_shape[0] * tile_shape[1],
            transcendentals=0,
        ),
        name="apply",
    )(pltpu.with_memory_space_constraint(tile, pltpu.HBM), to_all(lowered, "blk", blks))
    message = pl.pallas_call(
        pack_kernel,
        out_shape=jax.ShapeDtypeStruct((teams, PROBES + EXTRA, LANES), f32),
        in_specs=[pl.BlockSpec(memory_space=pltpu.SMEM)] + [VMEM] * 5,
        out_specs=VMEM,
        compiler_params=SMALL,
        name="pack",
    )(signal_var, partial, to_all(lowered, "team", teams), targets, applied, noise_var[None, :])
    total = jnp.sum(lax.all_to_all(message, "team", 0, 0), axis=0)
    twice = noise_var[None, :] * applied + weight * total[:PROBES]

    sums = jnp.sum(to_all(total[PROBES:], "blk", blks), axis=0)
    tt, ta, aa, ab = [sums[i, :PROBES, None] for i in range(4)]
    step_0 = tt / ta
    norm_1 = tt - 2.0 * step_0 * ta + step_0 * step_0 * aa
    ratio = norm_1 / tt
    curvature = (1 + ratio) * (1 + ratio) * ta - 2.0 * (1 + ratio) * step_0 * aa + step_0 * step_0 * ab
    step_1 = norm_1 / curvature
    residual = targets - step_0 * applied
    direction = residual + ratio * targets
    field = (1 + ratio) * applied - step_0 * twice
    return step_0 * targets + step_1 * direction, residual - step_1 * field


def solution(mesh):
    return jax.shard_map(
        shards,
        mesh=mesh,
        in_specs=(P(None, ("blk", "team")), P(), P(("blk", "team")), P(), P(None, ("blk", "team"))),
        out_specs=(P(None, ("blk", "team")), P(None, ("blk", "team"))),
        check_vma=False,
    )
```

time: 142 us -> 132 us (0.930)
  local copies, waits for them, and re-layouts: 14.5 us -> 2.83 us
  blocking collectives: 81 us -> 72.2 us
  starting transfers between devices: 16 us -> 22.4 us
  Pallas kernels: 12.9 us -> 17.8 us
  other arithmetic: 4.57 us -> 2.95 us
    unnamed x12 -> x4, local copies, waits for them, and re-layouts: 11.8 us -> 0.01 us
    all_to_all x4 -> x3, blocking collectives: 67.8 us -> 59 us  [to_all(): lax.all_to_all(jnp.broadcast_to(x[None], (size, *x.shape)), axis, 0, 0)]
    all_to_all x1 -> x2, starting transfers between devices: 10.2 us -> 16.6 us  [to_all(): lax.all_to_all(jnp.broadcast_to(x[None], (size, *x.shape)), axis, 0, 0)]
    pallas_call x2 -> x3, Pallas kernels: 12.9 us -> 17.8 us  [the longest x1 11.2 us: shards(): pl.pallas_call(lambda *refs: tile_kernel(*refs, deep=deep), out_shape=(pl...]
    all_to_all x1 -> x2, waiting for transfers between devices: 4.49 us -> 4.49 us  [to_all(): lax.all_to_all(jnp.broadcast_to(x[None], (size, *x.shape)), axis, 0, 0)]
  transfers between devices with their start and end apart: 2 -> 3, of which waited for: 2 -> 2; matrix products, arithmetic and copies ran while one was open for 1% -> 1% of each run, Pallas kernels for 0% -> 5%
where the time goes in v3:
time: 132 us; the launch traced here: 131 us
  blocking collectives  72.2 us (55%)
  starting transfers between devices  22.4 us (17%)
  Pallas kernels  17.8 us (13%)
  waiting for transfers between devices  11.1 us (8%)
  other arithmetic  2.95 us (2%)
  local copies, waits for them, and re-layouts  2.83 us (2%)
  between operations  1.38 us (1%)
    all_to_all x3, blocking collectives, to_all(): lax.all_to_all(jnp.broadcast_to(x[None], (size, *x.shape)), axis, 0, 0)  59 us
    all_to_all x2, starting transfers between devices, to_all(): lax.all_to_all(jnp.broadcast_to(x[None], (size, *x.shape)), axis, 0, 0)  16.6 us
    all_to_all x1, blocking collectives, shards(): total = jnp.sum(lax.all_to_all(message, 'team', 0, 0), axis=0)  13.3 us
    pallas_call x1, Pallas kernels, shards(): pl.pallas_call(lambda *refs: tile_kernel(*refs, deep=deep), out_shape=(pl...  11.2 us
    all_to_all x1, waiting for transfers between devices, shards(): total = jnp.sum(lax.all_to_all(partial, 'team', 0, 0), axis=0)  6.59 us
    pallas_call x1, Pallas kernels, shards(): pl.pallas_call(lambda *refs: apply_kernel(*refs, deep=deep), out_shape=ja...  6.41 us
    all_to_all x1, starting transfers between devices, shards(): total = jnp.sum(lax.all_to_all(partial, 'team', 0, 0), axis=0)  5.8 us
    all_to_all x2, waiting for transfers between devices, to_all(): lax.all_to_all(jnp.broadcast_to(x[None], (size, *x.shape)), axis, 0, 0)  4.49 us
  transfers between devices with their start and end apart: 3, of which 2 were waited for; matrix products, arithmetic and copies ran while one was open for 1% of the time, Pallas kernels for 5%

profile of v3, /device:TPU:1, one launch (start us, length us, event | category | flops | bytes accessed | tf_op | source)
XLA Modules:
  0.0 130.7 jit_solution(7605136214418158235)
XLA Ops:
  0.6 0.0 copy-start
  0.6 0.0 copy-start.1
  0.7 0.7 broadcast_in_dim.14.refs_0_
  1.4 1.3 %broadcast_in_dim.15 = bf16[16,16,128]{2,1,0:T(8,128)(2,1)} broadcast(bf16[16,128]{1,0:T(8,128)(2,1)} %param.5), dimensions={1,2} | broadcast | bytes 69632 | tf_op jit(solution)/shard_map/broadcast_in_dim | solution.py:128
  2.7 10.2 %all-to-all-start = ((bf16[16,16,128]{2,1,0:T(8,128)(2,1)}), bf16[16,16,128]{2,1,0:T(8,128)(2,1)S(1)}, u32[]{:S(2)}, u32[]{:S(2)}) async-start(bf16[16,16,128]{2,1,0:T(8,128)(2,1)} %broadcast_in_dim.15), calls=%async_computation | async-start | bytes 131072 | tf_op jit(solution)/shard_map/all_to_all | solution.py:128
  12.9 0.7 convert_element_type.6
  13.6 0.7 pad_maximum_fusion
  14.3 4.5 %all-to-all-done.refs_1_ = bf16[16,16,128]{2,1,0:T(8,128)(2,1)S(1)} async-done(((bf16[16,16,128]{2,1,0:T(8,128)(2,1)}), bf16[16,16,128]{2,1,0:T(8,128)(2,1)S(1)}, u32[]{:S(2)}, u32[]{:S(2)}) %all-to-all-start) | async-done | bytes 65568 | tf_op jit(solution)/shard_map/all_to_all | solution.py:128
  18.7 0.1 broadcast_in_dim.16
  18.8 26.7 %all_to_all.35.refs_2_ = bf16[32,48,128]{2,1,0:T(8,128)(2,1)S(1)} all-to-all(bf16[32,48,128]{2,1,0:T(8,128)(2,1)S(1)} %broadcast_in_dim.16), channel_id=1, replica_groups=mesh['blk'=32,'team'=16] {'blk'}, dimensions={0} | all-to-all | bytes 786432 | tf_op jit(solution)/shard_map/all_to_all | solution.py:128
  45.5 11.2 %tile.1 = (bf16[4096,2048]{1,0:T(8,128)(2,1)}, f32[16,32,128]{2,1,0:T(8,128)}) custom-call(f32[16,128]{1,0:T(8,128)S(1)} %broadcast_in_dim.14.refs_0_, bf16[16,16,128]{2,1,0:T(8,128)(2,1)S(1)} %all-to-all-done.refs_1_, bf16[32,48,128]{2,1,0:T(8,128)(2,1)S(1)} %all_to_all.35.refs_2_), custom_call_target="tpu_custom_call" | custom-call | tf_op jit(solution)/shard_map/tile/pallas_call | solution.py:138
  56.7 5.8 %all-to-all-start.2 = ((f32[16,32,128]{2,1,0:T(8,128)}), f32[16,32,128]{2,1,0:T(8,128)S(1)}, u32[]{:S(2)}, u32[]{:S(2)}) async-start(f32[16,32,128]{2,1,0:T(8,128)} %get-tuple-element.9), calls=%async_computation.2 | async-start | bytes 524288 | tf_op jit(solution)/shard_map/all_to_all | solution.py:153
  63.2 6.6 %all-to-all-done.2 = f32[16,32,128]{2,1,0:T(8,128)S(1)} async-done(((f32[16,32,128]{2,1,0:T(8,128)}), f32[16,32,128]{2,1,0:T(8,128)S(1)}, u32[]{:S(2)}, u32[]{:S(2)}) %all-to-all-start.2) | async-done | bytes 262176 | tf_op jit(solution)/shard_map/all_to_all | solution.py:153
  69.8 0.7 fusion.11
  70.5 16.5 %all_to_all.36.refs_1_ = bf16[32,32,128]{2,1,0:T(8,128)(2,1)S(1)} all-to-all(bf16[32,32,128]{2,1,0:T(8,128)(2,1)S(1)} %broadcast_in_dim.17), channel_id=1, replica_groups=mesh['blk'=32,'team'=16] {'blk'}, dimensions={0} | all-to-all | bytes 524288 | tf_op jit(solution)/shard_map/all_to_all | solution.py:128
  87.1 0.7 broadcast_in_dim.18
  87.8 6.4 %all-to-all-start.4 = ((bf16[16,32,128]{2,1,0:T(8,128)(2,1)}), bf16[16,32,128]{2,1,0:T(8,128)(2,1)S(1)}, u32[]{:S(2)}, u32[]{:S(2)}) async-start(bf16[16,32,128]{2,1,0:T(8,128)(2,1)} %broadcast_in_dim.18), calls=%async_computation.4 | async-start | bytes 262144 | tf_op jit(solution)/shard_map/all_to_all | solution.py:128
  94.2 6.4 %apply.1.partial_ref = f32[16,32,128]{2,1,0:T(8,128)S(1)} custom-call(bf16[4096,2048]{1,0:T(8,128)(2,1)} %get-tuple-element.8.refs_0_, bf16[32,32,128]{2,1,0:T(8,128)(2,1)S(1)} %all_to_all.36.refs_1_), custom_call_target="tpu_custom_call" | custom-call | flops 536870912 | bytes 16777216 | tf_op jit(solution)/shard_map/apply/pallas_call | solution.py:156
  100.6 0.0 all-to-all-done.4.cols_ref
  100.6 0.0 copy-done
  100.6 0.0 copy-done.1
  100.6 0.2 pack.1
  100.8 13.3 %all_to_all.37 = f32[16,40,128]{2,1,0:T(8,128)S(1)} all-to-all(f32[16,40,128]{2,1,0:T(8,128)S(1)} %pack.1), channel_id=1, replica_groups=mesh['blk'=32,'team'=16] {'team'}, dimensions={0} | all-to-all | bytes 655360 | tf_op jit(solution)/shard_map/all_to_all | solution.py:178
  114.1 15.7 %all_to_all.38 = f32[32,8,128]{2,1,0:T(8,128)S(1)} all-to-all(f32[32,8,128]{2,1,0:T(8,128)S(1)} %broadcast_in_dim.20), channel_id=1, replica_groups=mesh['blk'=32,'team'=16] {'blk'}, dimensions={0} | all-to-all | bytes 262144 | tf_op jit(solution)/shard_map/all_to_all | solution.py:128
  130.0 0.7 fusion.4
  (8 shorter events, 0.2 us)
Async XLA Ops:
  0.6 100.0 %copy-start = (f32[32,128]{1,0:T(8,128)S(1)}, f32[32,128]{1,0:T(8,128)}, u32[]{:S(2)}) copy-start(f32[32,128]{1,0:T(8,128)} %targets_ref.1) | copy-start | bytes 49156
  0.6 100.0 %copy-start.1 = (f32[128]{0:T(128)S(1)}, f32[128]{0:T(128)}, u32[]{:S(2)}) copy-start(f32[128]{0:T(128)} %param.7) | copy-start | bytes 1540
  2.7 16.0 %all-to-all-start = ((bf16[16,16,128]{2,1,0:T(8,128)(2,1)}), bf16[16,16,128]{2,1,0:T(8,128)(2,1)S(1)}, u32[]{:S(2)}, u32[]{:S(2)}) async-start(bf16[16,16,128]{2,1,0:T(8,128)(2,1)} %broadcast_in_dim.15), calls=%async_computation | async-start | bytes 131072 | tf_op jit(solution)/shard_map/all_to_all | solution.py:128
  56.7 13.0 %all-to-all-start.2 = ((f32[16,32,128]{2,1,0:T(8,128)}), f32[16,32,128]{2,1,0:T(8,128)S(1)}, u32[]{:S(2)}, u32[]{:S(2)}) async-start(f32[16,32,128]{2,1,0:T(8,128)} %get-tuple-element.9), calls=%async_computation.2 | async-start | bytes 524288 | tf_op jit(solution)/shard_map/all_to_all | solution.py:153
  87.8 12.9 %all-to-all-start.4 = ((bf16[16,32,128]{2,1,0:T(8,128)(2,1)}), bf16[16,32,128]{2,1,0:T(8,128)(2,1)S(1)}, u32[]{:S(2)}, u32[]{:S(2)}) async-start(bf16[16,32,128]{2,1,0:T(8,128)(2,1)} %broadcast_in_dim.18), calls=%async_computation.4 | async-start | bytes 262144 | tf_op jit(solution)/shard_map/all_to_all | solution.py:128

commit v4 on v3

v4 whole, which is shorter than its diff:
```python
import math

import jax
import jax.numpy as jnp
from jax import lax
from jax.experimental import pallas as pl
from jax.experimental.pallas import tpu as pltpu
from jax.sharding import PartitionSpec as P

f32, bf16 = jnp.float32, jnp.bfloat16
DIMS, PROBES, LANES = 16, 32, 128
FEATURES = 4 * DIMS
EXTRA = 8
LOG2E = math.log2(math.e)
VMEM = pl.BlockSpec(memory_space=pltpu.VMEM)
SMEM = pl.BlockSpec(memory_space=pltpu.SMEM)
HBM = pl.BlockSpec(memory_space=pltpu.HBM)
LARGE = pltpu.CompilerParams(vmem_limit_bytes=24 * 2**20)
SMALL = pltpu.CompilerParams(vmem_limit_bytes=8 * 2**20)


def pieces(x):
    hi = x.astype(bf16).astype(f32)
    rest = x - hi
    mid = rest.astype(bf16).astype(f32)
    low = (rest - mid).astype(bf16).astype(f32)
    return hi, mid, low


def features(parts, halves):
    row = lax.broadcasted_iota(jnp.int32, (DIMS, LANES), 0)
    extra = jnp.zeros((DIMS, LANES), f32)
    for place, values in enumerate(halves):
        extra = jnp.where(row == place, jnp.broadcast_to(values, extra.shape), extra)
    return jnp.concatenate([*parts, extra], axis=0)


def half_norms(points, inv_scale):
    scaled = points * inv_scale
    return pieces((-0.5 * LOG2E) * jnp.sum(scaled * scaled, axis=0, keepdims=True))


def tile_kernel(
    inv_scale_ref, cols_ref, rows_ref, field_ref, noise_ref,
    tile_ref, tail_ref, partial_ref, field_out_ref, noise_out_ref,
    lhs, rhs, held, sems, more_sems,
):
    copies = [
        pltpu.make_async_copy(field_ref, field_out_ref, more_sems.at[0]),
        pltpu.make_async_copy(noise_ref, noise_out_ref, more_sems.at[1]),
    ]
    for copy in copies:
        copy.start()
    inv_scale = inv_scale_ref[...]
    n_cols, n_rows = cols_ref.shape[0], rows_ref.shape[0]
    deep = tail_ref.shape[0]
    one = jnp.ones((1, LANES), f32)
    for i in range(n_cols):
        points = cols_ref[i].astype(f32)
        block = features((points, points, points), (*half_norms(points, inv_scale), one, one, one))
        rhs[:, i * LANES : (i + 1) * LANES] = block.astype(bf16)
    for i in range(n_rows):
        points = rows_ref[i, :DIMS, :].astype(f32)
        weighted = points * (inv_scale * inv_scale * LOG2E)
        block = features(pieces(weighted), (one, one, one, *half_norms(points, inv_scale)))
        lhs[i * LANES : (i + 1) * LANES, :] = block.T.astype(bf16)

    total = jnp.zeros((PROBES, n_cols * LANES), f32)
    for j, start in enumerate(range(0, n_rows * LANES, deep)):
        here = slice(start, start + deep)
        exponent = jnp.dot(lhs[here, :], rhs[...], preferred_element_type=f32)
        block = jnp.exp2(exponent).astype(bf16)
        if start + deep < n_rows * LANES:
            held[here, :] = block
            copies.append(pltpu.make_async_copy(held.at[here, :], tile_ref.at[here, :], sems.at[j]))
            copies[-1].start()
        else:
            tail_ref[...] = block
        v = jnp.concatenate([rows_ref[m, DIMS:, :] for m in range(start // LANES, (start + deep) // LANES)], axis=1)
        total = total + jnp.dot(v, block, preferred_element_type=f32)
    for m in range(n_cols):
        partial_ref[m] = total[:, m * LANES : (m + 1) * LANES]
    for copy in copies:
        copy.wait()


def combine_kernel(weight_ref, received_ref, field_ref, noise_ref, applied_ref, to_blk_ref, to_team_ref):
    total = received_ref[0]
    for m in range(1, received_ref.shape[0]):
        total = total + received_ref[m]
    applied = noise_ref[...] * field_ref[...] + weight_ref[0] * total
    applied_ref[...] = applied
    lowered = applied.astype(bf16)
    for copies_ref in (to_blk_ref, to_team_ref):
        for m in range(copies_ref.shape[0]):
            copies_ref[m] = lowered


def apply_kernel(tile_ref, tail_ref, v_ref, partial_ref, held, sems):
    deep, rows = tail_ref.shape[0], tile_ref.shape[0]

    def product(start, block):
        v = jnp.concatenate([v_ref[m] for m in range(start // LANES, (start + deep) // LANES)], axis=1)
        return jnp.dot(v, block, preferred_element_type=f32)

    copies = []
    for j, start in enumerate(range(0, rows, deep)):
        here = slice(start, start + deep)
        copies.append((start, pltpu.make_async_copy(tile_ref.at[here, :], held.at[here, :], sems.at[j])))
        copies[-1][1].start()
    total = product(rows, tail_ref[...])
    for start, copy in copies:
        copy.wait()
        total = total + product(start, held[start : start + deep, :])
    for m in range(partial_ref.shape[0]):
        partial_ref[m] = total[:, m * LANES : (m + 1) * LANES]


def pack_kernel(weight_ref, partial_ref, cols_ref, targets_ref, applied_ref, noise_ref, message_ref):
    targets, applied = targets_ref[...], applied_ref[...]
    inner = jnp.zeros(targets.shape, f32)
    for m in range(partial_ref.shape[0]):
        message_ref[m, :PROBES, :] = partial_ref[m]
        inner = inner + cols_ref[m].astype(f32) * partial_ref[m]
    inner = weight_ref[0] * inner + noise_ref[...] * applied * applied
    lane = lax.broadcasted_iota(jnp.int32, (PROBES, LANES), 1)
    sums = jnp.zeros((PROBES, LANES), f32)
    for place, product in enumerate((targets * targets, targets * applied, applied * applied, inner)):
        sums = jnp.where(lane == place, jnp.sum(product, axis=1, keepdims=True), sums)
    sums = jnp.concatenate([sums, jnp.zeros((LANES - PROBES, LANES), f32)], axis=0).T[:EXTRA]
    for m in range(partial_ref.shape[0]):
        message_ref[m, PROBES:, :] = sums


def in_hbm(x):
    return pltpu.with_memory_space_constraint(x, pltpu.HBM)


def shards(points, inv_scale, noise_var, signal_var, targets):
    blks, teams = lax.axis_size("blk"), lax.axis_size("team")

    def to_all(x, axis, size):
        return lax.all_to_all(jnp.broadcast_to(x[None], (size, *x.shape)), axis, 0, 0)

    cols = to_all(points, "team", teams)
    own = jnp.concatenate([points, targets.astype(bf16)], axis=0)
    own, inv_scale = lax.optimization_barrier((own, jnp.broadcast_to(inv_scale[:, None], (DIMS, LANES))))
    rows = to_all(own, "blk", blks)
    deep, wide = 512, teams * LANES
    tile_shape = (blks * LANES - deep, wide)
    sems = pltpu.SemaphoreType.DMA((tile_shape[0] // deep,))
    tile, tail, partial, field, noise = pl.pallas_call(
        tile_kernel,
        out_shape=(
            pltpu.HBM(tile_shape, bf16),
            jax.ShapeDtypeStruct((deep, wide), bf16),
            jax.ShapeDtypeStruct((teams, PROBES, LANES), f32),
            jax.ShapeDtypeStruct((PROBES, LANES), f32),
            jax.ShapeDtypeStruct((1, LANES), f32),
        ),
        in_specs=[VMEM] * 3 + [HBM] * 2,
        out_specs=[HBM] + [VMEM] * 4,
        scratch_shapes=[
            pltpu.VMEM((blks * LANES, FEATURES), bf16),
            pltpu.VMEM((FEATURES, wide), bf16),
            pltpu.VMEM(tile_shape, bf16),
            sems,
            pltpu.SemaphoreType.DMA((2,)),
        ],
        compiler_params=LARGE,
        name="tile",
    )(inv_scale, cols, rows, in_hbm(targets), in_hbm(noise_var[None, :]))

    applied, to_blk, to_team = pl.pallas_call(
        combine_kernel,
        out_shape=(
            jax.ShapeDtypeStruct((PROBES, LANES), f32),
            jax.ShapeDtypeStruct((blks, PROBES, LANES), bf16),
            jax.ShapeDtypeStruct((teams, PROBES, LANES), bf16),
        ),
        in_specs=[SMEM] + [VMEM] * 3,
        out_specs=[VMEM] * 3,
        compiler_params=SMALL,
        name="combine",
    )(signal_var, lax.all_to_all(partial, "team", 0, 0), field, noise)
    partial = pl.pallas_call(
        apply_kernel,
        out_shape=jax.ShapeDtypeStruct((teams, PROBES, LANES), f32),
        in_specs=[HBM, VMEM, VMEM],
        out_specs=VMEM,
        scratch_shapes=[pltpu.VMEM(tile_shape, bf16), sems],
        compiler_params=LARGE,
        cost_estimate=pl.CostEstimate(
            flops=2 * PROBES * tile_shape[0] * tile_shape[1],
            bytes_accessed=2 * tile_shape[0] * tile_shape[1],
            transcendentals=0,
        ),
        name="apply",
    )(in_hbm(tile), tail, lax.all_to_all(to_blk, "blk", 0, 0))
    message = pl.pallas_call(
        pack_kernel,
        out_shape=jax.ShapeDtypeStruct((teams, PROBES + EXTRA, LANES), f32),
        in_specs=[SMEM] + [VMEM] * 5,
        out_specs=VMEM,
        compiler_params=SMALL,
        name="pack",
    )(signal_var, partial, lax.all_to_all(to_team, "team", 0, 0), field, applied, noise)
    total = jnp.sum(lax.all_to_all(message, "team", 0, 0), axis=0)
    twice = noise * applied + signal_var[0] * total[:PROBES]

    sums = jnp.sum(to_all(total[PROBES:], "blk", blks), axis=0)
    tt, ta, aa, ab = [sums[i, :PROBES, None] for i in range(4)]
    step_0 = tt / ta
    norm_1 = tt - 2.0 * step_0 * ta + step_0 * step_0 * aa
    ratio = norm_1 / tt
    curvature = (1 + ratio) * (1 + ratio) * ta - 2.0 * (1 + ratio) * step_0 * aa + step_0 * step_0 * ab
    step_1 = norm_1 / curvature
    residual = field - step_0 * applied
    direction = residual + ratio * field
    slope = (1 + ratio) * applied - step_0 * twice
    return step_0 * field + step_1 * direction, residual - step_1 * slope


def solution(mesh):
    return jax.shard_map(
        shards,
        mesh=mesh,
        in_specs=(P(None, ("blk", "team")), P(), P(("blk", "team")), P(), P(None, ("blk", "team"))),
        out_specs=(P(None, ("blk", "team")), P(None, ("blk", "team"))),
        check_vma=False,
    )
```

time: 132 us -> 127 us (0.962)
  Pallas kernels: 17.8 us -> 15.2 us
    all_to_all x3 -> x2, blocking collectives: 59 us -> 42.4 us  [to_all(): lax.all_to_all(jnp.broadcast_to(x[None], (size, *x.shape)), axis, 0, 0)]
    all_to_all x0 -> x1, blocking collectives: none -> 16.5 us  [shards(): lax.all_to_all(to_blk, 'blk', 0, 0)]
    all_to_all x1 -> x2, starting transfers between devices: 5.8 us -> 12.2 us  [the longest x1 6.43 us: shards(): lax.all_to_all(to_team, 'team', 0, 0)]
    all_to_all x2 -> x1, starting transfers between devices: 16.6 us -> 10.2 us  [to_all(): lax.all_to_all(jnp.broadcast_to(x[None], (size, *x.shape)), axis, 0, 0)]
    pallas_call x2 -> x3, Pallas kernels: 17.6 us -> 15 us  [the longest x1 8.53 us: shards(): pl.pallas_call(tile_kernel, out_shape=(pltpu.HBM(tile_shape, bf16), jax.S...]
    all_to_all x2 -> x1, waiting for transfers between devices: 4.49 us -> 3.76 us  [to_all(): lax.all_to_all(jnp.broadcast_to(x[None], (size, *x.shape)), axis, 0, 0)]
    all_to_all x1 -> x2, waiting for transfers between devices: 6.59 us -> 7.02 us  [the longest x1 6.59 us: shards(): lax.all_to_all(partial, 'team', 0, 0)]
  transfers between devices with their start and end apart: 3 -> 3, of which waited for: 2 -> 3; matrix products, arithmetic and copies ran while one was open for 1% -> 2% of each run, Pallas kernels for 5% -> 5%
where the time goes in v4:
time: 127 us; the launch traced here: 126 us
  blocking collectives  71.8 us (57%)
  starting transfers between devices  22.4 us (18%)
  Pallas kernels  15.2 us (12%)
  waiting for transfers between devices  10.8 us (9%)
  other arithmetic  2.2 us (2%)
  local copies, waits for them, and re-layouts  2.11 us (2%)
  between operations  1.33 us (1%)
    all_to_all x2, blocking collectives, to_all(): lax.all_to_all(jnp.broadcast_to(x[None], (size, *x.shape)), axis, 0, 0)  42.4 us
    all_to_all x1, blocking collectives, shards(): lax.all_to_all(to_blk, 'blk', 0, 0)  16.5 us
    all_to_all x1, blocking collectives, shards(): total = jnp.sum(lax.all_to_all(message, 'team', 0, 0), axis=0)  12.8 us
    all_to_all x1, starting transfers between devices, to_all(): lax.all_to_all(jnp.broadcast_to(x[None], (size, *x.shape)), axis, 0, 0)  10.2 us
    pallas_call x1, Pallas kernels, shards(): pl.pallas_call(tile_kernel, out_shape=(pltpu.HBM(tile_shape, bf16), jax.S...  8.53 us
    all_to_all x1, waiting for transfers between devices, shards(): lax.all_to_all(partial, 'team', 0, 0)  6.59 us
    all_to_all x1, starting transfers between devices, shards(): lax.all_to_all(to_team, 'team', 0, 0)  6.43 us
    all_to_all x1, starting transfers between devices, shards(): lax.all_to_all(partial, 'team', 0, 0)  5.79 us
  transfers between devices with their start and end apart: 3, of which 3 were waited for; matrix products, arithmetic and copies ran while one was open for 2% of the time, Pallas kernels for 5%

profile of v4, /device:TPU:1, one launch (start us, length us, event | category | flops | bytes accessed | tf_op | source)
XLA Modules:
  0.0 125.8 jit_solution(12377651016288214379)
XLA Ops:
  0.6 1.3 %broadcast_in_dim.11 = bf16[16,16,128]{2,1,0:T(8,128)(2,1)} broadcast(bf16[16,128]{1,0:T(8,128)(2,1)} %param.5), dimensions={1,2} | broadcast | bytes 69632 | tf_op jit(solution)/shard_map/broadcast_in_dim | solution.py:143
  1.9 10.2 %all-to-all-start = ((bf16[16,16,128]{2,1,0:T(8,128)(2,1)}), bf16[16,16,128]{2,1,0:T(8,128)(2,1)S(1)}, u32[]{:S(2)}, u32[]{:S(2)}) async-start(bf16[16,16,128]{2,1,0:T(8,128)(2,1)} %broadcast_in_dim.11), calls=%async_computation | async-start | bytes 131072 | tf_op jit(solution)/shard_map/all_to_all | solution.py:143
  12.1 0.7 convert_element_type.3
  12.8 0.7 pad_maximum_fusion
  13.5 0.7 broadcast_in_dim.10.inv_scale_ref
  14.2 3.8 %all-to-all-done.cols_ref = bf16[16,16,128]{2,1,0:T(8,128)(2,1)S(1)} async-done(((bf16[16,16,128]{2,1,0:T(8,128)(2,1)}), bf16[16,16,128]{2,1,0:T(8,128)(2,1)S(1)}, u32[]{:S(2)}, u32[]{:S(2)}) %all-to-all-start) | async-done | bytes 65568 | tf_op jit(solution)/shard_map/all_to_all | solution.py:143
  18.0 0.1 broadcast_in_dim.12
  18.1 26.7 %all_to_all.35.rows_ref = bf16[32,48,128]{2,1,0:T(8,128)(2,1)S(1)} all-to-all(bf16[32,48,128]{2,1,0:T(8,128)(2,1)S(1)} %broadcast_in_dim.12), channel_id=1, replica_groups=mesh['blk'=32,'team'=16] {'blk'}, dimensions={0} | all-to-all | bytes 786432 | tf_op jit(solution)/shard_map/all_to_all | solution.py:143
  44.7 8.5 %tile.1 = (bf16[3584,2048]{1,0:T(8,128)(2,1)}, bf16[512,2048]{1,0:T(8,128)(2,1)S(1)}, f32[16,32,128]{2,1,0:T(8,128)}, f32[32,128]{1,0:T(8,128)S(1)}, f32[1,128]{1,0:T(1,128)S(1)}) custom-call(f32[16,128]{1,0:T(8,128)S(1)} %broadcast_in_dim.10.inv_scale_ref, bf16[16,16,128]{2,1,0:T(8,128)(2,1)S(1)} %all-to-all-done.cols_ref, ...), custom_call_target="tpu_custom_call" | custom-call | tf_op jit(solution)/shard_map/tile/pallas_call | solution.py:152
  53.3 5.8 %all-to-all-start.2 = ((f32[16,32,128]{2,1,0:T(8,128)}), f32[16,32,128]{2,1,0:T(8,128)S(1)}, u32[]{:S(2)}, u32[]{:S(2)}) async-start(f32[16,32,128]{2,1,0:T(8,128)} %get-tuple-element.16), calls=%async_computation.2 | async-start | bytes 524288 | tf_op jit(solution)/shard_map/all_to_all | solution.py:185
  59.7 6.6 %all-to-all-done.2.received_ref = f32[16,32,128]{2,1,0:T(8,128)S(1)} async-done(((f32[16,32,128]{2,1,0:T(8,128)}), f32[16,32,128]{2,1,0:T(8,128)S(1)}, u32[]{:S(2)}, u32[]{:S(2)}) %all-to-all-start.2) | async-done | bytes 262176 | tf_op jit(solution)/shard_map/all_to_all | solution.py:185
  66.3 0.7 combine.1
  67.0 16.5 %all_to_all.36.v_ref = bf16[32,32,128]{2,1,0:T(8,128)(2,1)S(1)} all-to-all(bf16[32,32,128]{2,1,0:T(8,128)(2,1)S(1)} %get-tuple-element.19), channel_id=1, replica_groups=mesh['blk'=32,'team'=16] {'blk'}, dimensions={0} | all-to-all | bytes 524288 | tf_op jit(solution)/shard_map/all_to_all | solution.py:199
  83.5 6.4 %all-to-all-start.4 = ((bf16[16,32,128]{2,1,0:T(8,128)(2,1)}), bf16[16,32,128]{2,1,0:T(8,128)(2,1)S(1)}, u32[]{:S(2)}, u32[]{:S(2)}) async-start(bf16[16,32,128]{2,1,0:T(8,128)(2,1)} %get-tuple-element.20), calls=%async_computation.4 | async-start | bytes 262144 | tf_op jit(solution)/shard_map/all_to_all | solution.py:207
  90.0 5.8 %apply.1.partial_ref = f32[16,32,128]{2,1,0:T(8,128)S(1)} custom-call(bf16[3584,2048]{1,0:T(8,128)(2,1)} %get-tuple-element.14.tile_ref, bf16[512,2048]{1,0:T(8,128)(2,1)S(1)} %get-tuple-element.15.tail_ref, bf16[32,32,128]{2,1,0:T(8,128)(2,1)S(1)} %all_to_all.36.v_ref), custom_call_target="tpu_custom_call" | custom-call | flops 469762048 | bytes 14680064 | tf_op jit(solution)/shard_map/apply/pallas_call | solution.py:186
  95.8 0.4 all-to-all-done.4.cols_ref
  96.2 0.2 pack.1
  96.4 12.8 %all_to_all.37 = f32[16,40,128]{2,1,0:T(8,128)S(1)} all-to-all(f32[16,40,128]{2,1,0:T(8,128)S(1)} %pack.1), channel_id=1, replica_groups=mesh['blk'=32,'team'=16] {'team'}, dimensions={0} | all-to-all | bytes 655360 | tf_op jit(solution)/shard_map/all_to_all | solution.py:208
  109.3 15.7 %all_to_all.38 = f32[32,8,128]{2,1,0:T(8,128)S(1)} all-to-all(f32[32,8,128]{2,1,0:T(8,128)S(1)} %broadcast_in_dim.14), channel_id=1, replica_groups=mesh['blk'=32,'team'=16] {'blk'}, dimensions={0} | all-to-all | bytes 262144 | tf_op jit(solution)/shard_map/all_to_all | solution.py:143
  125.1 0.7 fusion.4
  (6 shorter events, 0.1 us)
Async XLA Ops:
  1.9 16.1 %all-to-all-start = ((bf16[16,16,128]{2,1,0:T(8,128)(2,1)}), bf16[16,16,128]{2,1,0:T(8,128)(2,1)S(1)}, u32[]{:S(2)}, u32[]{:S(2)}) async-start(bf16[16,16,128]{2,1,0:T(8,128)(2,1)} %broadcast_in_dim.11), calls=%async_computation | async-start | bytes 131072 | tf_op jit(solution)/shard_map/all_to_all | solution.py:143
  53.3 13.0 %all-to-all-start.2 = ((f32[16,32,128]{2,1,0:T(8,128)}), f32[16,32,128]{2,1,0:T(8,128)S(1)}, u32[]{:S(2)}, u32[]{:S(2)}) async-start(f32[16,32,128]{2,1,0:T(8,128)} %get-tuple-element.16), calls=%async_computation.2 | async-start | bytes 524288 | tf_op jit(solution)/shard_map/all_to_all | solution.py:185
  83.5 12.7 %all-to-all-start.4 = ((bf16[16,32,128]{2,1,0:T(8,128)(2,1)}), bf16[16,32,128]{2,1,0:T(8,128)(2,1)S(1)}, u32[]{:S(2)}, u32[]{:S(2)}) async-start(bf16[16,32,128]{2,1,0:T(8,128)(2,1)} %get-tuple-element.20), calls=%async_computation.4 | async-start | bytes 262144 | tf_op jit(solution)/shard_map/all_to_all | solution.py:207

commit v5 on v4

--- a/solution.py
+++ b/solution.py
@@ -10,10 +10,9 @@
 f32, bf16 = jnp.float32, jnp.bfloat16
 DIMS, PROBES, LANES = 16, 32, 128
 FEATURES = 4 * DIMS
-EXTRA = 8
+EXTRA = 16
 LOG2E = math.log2(math.e)
 VMEM = pl.BlockSpec(memory_space=pltpu.VMEM)
-SMEM = pl.BlockSpec(memory_space=pltpu.SMEM)
 HBM = pl.BlockSpec(memory_space=pltpu.HBM)
 LARGE = pltpu.CompilerParams(vmem_limit_bytes=24 * 2**20)
 SMALL = pltpu.CompilerParams(vmem_limit_bytes=8 * 2**20)
@@ -88,7 +87,7 @@
     total = received_ref[0]
     for m in range(1, received_ref.shape[0]):
         total = total + received_ref[m]
-    applied = noise_ref[...] * field_ref[...] + weight_ref[0] * total
+    applied = noise_ref[...] * field_ref[...] + weight_ref[...] * total
     applied_ref[...] = applied
     lowered = applied.astype(bf16)
     for copies_ref in (to_blk_ref, to_team_ref):
@@ -120,14 +119,15 @@
     targets, applied = targets_ref[...], applied_ref[...]
     inner = jnp.zeros(targets.shape, f32)
     for m in range(partial_ref.shape[0]):
-        message_ref[m, :PROBES, :] = partial_ref[m]
+        message_ref[m, :PROBES, :] = partial_ref[m].astype(bf16)
         inner = inner + cols_ref[m].astype(f32) * partial_ref[m]
-    inner = weight_ref[0] * inner + noise_ref[...] * applied * applied
+    inner = weight_ref[...] * inner + noise_ref[...] * applied * applied
     lane = lax.broadcasted_iota(jnp.int32, (PROBES, LANES), 1)
     sums = jnp.zeros((PROBES, LANES), f32)
     for place, product in enumerate((targets * targets, targets * applied, applied * applied, inner)):
-        sums = jnp.where(lane == place, jnp.sum(product, axis=1, keepdims=True), sums)
-    sums = jnp.concatenate([sums, jnp.zeros((LANES - PROBES, LANES), f32)], axis=0).T[:EXTRA]
+        for piece, part in enumerate(pieces(jnp.sum(product, axis=1, keepdims=True))):
+            sums = jnp.where(lane == 4 * piece + place, part, sums)
+    sums = jnp.concatenate([sums, jnp.zeros((LANES - PROBES, LANES), f32)], axis=0).T[:EXTRA].astype(bf16)
     for m in range(partial_ref.shape[0]):
         message_ref[m, PROBES:, :] = sums
 
@@ -144,7 +144,9 @@
 
     cols = to_all(points, "team", teams)
     own = jnp.concatenate([points, targets.astype(bf16)], axis=0)
-    own, inv_scale = lax.optimization_barrier((own, jnp.broadcast_to(inv_scale[:, None], (DIMS, LANES))))
+    own, inv_scale, weight = lax.optimization_barrier(
+        (own, jnp.broadcast_to(inv_scale[:, None], (DIMS, LANES)), jnp.broadcast_to(signal_var[None], (1, LANES)))
+    )
     rows = to_all(own, "blk", blks)
     deep, wide = 512, teams * LANES
     tile_shape = (blks * LANES - deep, wide)
@@ -178,11 +180,11 @@
             jax.ShapeDtypeStruct((blks, PROBES, LANES), bf16),
             jax.ShapeDtypeStruct((teams, PROBES, LANES), bf16),
         ),
-        in_specs=[SMEM] + [VMEM] * 3,
+        in_specs=[VMEM] + [VMEM] * 3,
         out_specs=[VMEM] * 3,
         compiler_params=SMALL,
         name="combine",
-    )(signal_var, lax.all_to_all(partial, "team", 0, 0), field, noise)
+    )(weight, lax.all_to_all(partial, "team", 0, 0), field, noise)
     partial = pl.pallas_call(
         apply_kernel,
         out_shape=jax.ShapeDtypeStruct((teams, PROBES, LANES), f32),
@@ -199,17 +201,18 @@
     )(in_hbm(tile), tail, lax.all_to_all(to_blk, "blk", 0, 0))
     message = pl.pallas_call(
         pack_kernel,
-        out_shape=jax.ShapeDtypeStruct((teams, PROBES + EXTRA, LANES), f32),
-        in_specs=[SMEM] + [VMEM] * 5,
+        out_shape=jax.ShapeDtypeStruct((teams, PROBES + EXTRA, LANES), bf16),
+        in_specs=[VMEM] + [VMEM] * 5,
         out_specs=VMEM,
         compiler_params=SMALL,
         name="pack",
-    )(signal_var, partial, lax.all_to_all(to_team, "team", 0, 0), field, applied, noise)
-    total = jnp.sum(lax.all_to_all(message, "team", 0, 0), axis=0)
-    twice = noise * applied + signal_var[0] * total[:PROBES]
-
-    sums = jnp.sum(to_all(total[PROBES:], "blk", blks), axis=0)
-    tt, ta, aa, ab = [sums[i, :PROBES, None] for i in range(4)]
+    )(weight, partial, lax.all_to_all(to_team, "team", 0, 0), field, applied, noise)
+    total = jnp.sum(lax.all_to_all(message, "team", 0, 0).astype(f32), axis=0)
+    twice = noise * applied + weight * total[:PROBES]
+
+    sums = total[PROBES : PROBES + 8] + total[PROBES + 8 :]
+    sums = jnp.sum(to_all(sums, "blk", blks), axis=0)
+    tt, ta, aa, ab = [(sums[i] + sums[i + 4])[:PROBES, None] for i in range(4)]
     step_0 = tt / ta
     norm_1 = tt - 2.0 * step_0 * ta + step_0 * step_0 * aa
     ratio = norm_1 / tt

time: 127 us -> 124 us (0.976)
  blocking collectives: 71.8 us -> 82.9 us
  waiting for transfers between devices: 10.8 us -> 3.53 us
  starting transfers between devices: 22.4 us -> 16.6 us
    all_to_all x1 -> x2, blocking collectives: 12.8 us -> 24 us  [the longest x1 12.1 us: shards(): lax.all_to_all(partial, 'team', 0, 0)]
    all_to_all x1 -> x0, waiting for transfers between devices: 6.59 us -> none  [shards(): lax.all_to_all(partial, 'team', 0, 0)]
    all_to_all x1 -> x0, starting transfers between devices: 5.79 us -> none  [shards(): lax.all_to_all(partial, 'team', 0, 0)]
  transfers between devices with their start and end apart: 3 -> 2, of which waited for: 3 -> 2; matrix products, arithmetic and copies ran while one was open for 2% -> 2% of each run, Pallas kernels for 5% -> 5%
where the time goes in v5:
time: 124 us; the launch traced here: 123 us
  blocking collectives  82.9 us (67%)
  starting transfers between devices  16.6 us (13%)
  Pallas kernels  14.4 us (12%)
  waiting for transfers between devices  3.53 us (3%)
  other arithmetic  2.22 us (2%)
  local copies, waits for them, and re-layouts  2.1 us (2%)
  between operations  1.33 us (1%)
    all_to_all x2, blocking collectives, to_all(): lax.all_to_all(jnp.broadcast_to(x[None], (size, *x.shape)), axis, 0, 0)  42.4 us
    all_to_all x1, blocking collectives, shards(): lax.all_to_all(to_blk, 'blk', 0, 0)  16.5 us
    all_to_all x1, blocking collectives, shards(): lax.all_to_all(partial, 'team', 0, 0)  12.1 us
    all_to_all x1, blocking collectives, shards(): total = jnp.sum(lax.all_to_all(message, 'team', 0, 0).astype(f32), axis=0)  11.8 us
    all_to_all x1, starting transfers between devices, to_all(): lax.all_to_all(jnp.broadcast_to(x[None], (size, *x.shape)), axis, 0, 0)  10.2 us
    pallas_call x1, Pallas kernels, shards(): pl.pallas_call(tile_kernel, out_shape=(pltpu.HBM(tile_shape, bf16), jax.S...  7.68 us
    all_to_all x1, starting transfers between devices, shards(): lax.all_to_all(to_team, 'team', 0, 0)  6.43 us
    pallas_call x1, Pallas kernels, shards(): pl.pallas_call(apply_kernel, out_shape=jax.ShapeDtypeStruct((teams, PROBE...  5.79 us
  transfers between devices with their start and end apart: 2, of which 2 were waited for; matrix products, arithmetic and copies ran while one was open for 2% of the time, Pallas kernels for 5%

profile of v5, /device:TPU:1, one launch (start us, length us, event | category | flops | bytes accessed | tf_op | source)
XLA Modules:
  0.0 123.1 jit_solution(8586075053865960119)
XLA Ops:
  0.6 1.3 %broadcast_in_dim.17 = bf16[16,16,128]{2,1,0:T(8,128)(2,1)} broadcast(bf16[16,128]{1,0:T(8,128)(2,1)} %param.5), dimensions={1,2} | broadcast | bytes 69632 | tf_op jit(solution)/shard_map/broadcast_in_dim | solution.py:143
  1.9 10.2 %all-to-all-start = ((bf16[16,16,128]{2,1,0:T(8,128)(2,1)}), bf16[16,16,128]{2,1,0:T(8,128)(2,1)S(1)}, u32[]{:S(2)}, u32[]{:S(2)}) async-start(bf16[16,16,128]{2,1,0:T(8,128)(2,1)} %broadcast_in_dim.17), calls=%async_computation | async-start | bytes 131072 | tf_op jit(solution)/shard_map/all_to_all | solution.py:143
  12.7 0.7 convert_element_type.6
  13.5 0.7 pad_maximum_fusion
  14.2 0.7 broadcast_in_dim.14.inv_scale_ref
  14.9 3.1 %all-to-all-done.cols_ref = bf16[16,16,128]{2,1,0:T(8,128)(2,1)S(1)} async-done(((bf16[16,16,128]{2,1,0:T(8,128)(2,1)}), bf16[16,16,128]{2,1,0:T(8,128)(2,1)S(1)}, u32[]{:S(2)}, u32[]{:S(2)}) %all-to-all-start) | async-done | bytes 65568 | tf_op jit(solution)/shard_map/all_to_all | solution.py:143
  18.0 0.1 broadcast_in_dim.18
  18.0 26.7 %all_to_all.35.rows_ref = bf16[32,48,128]{2,1,0:T(8,128)(2,1)S(1)} all-to-all(bf16[32,48,128]{2,1,0:T(8,128)(2,1)S(1)} %broadcast_in_dim.18), channel_id=1, replica_groups=mesh['blk'=32,'team'=16] {'blk'}, dimensions={0} | all-to-all | bytes 786432 | tf_op jit(solution)/shard_map/all_to_all | solution.py:143
  44.7 7.7 %tile.1 = (bf16[3584,2048]{1,0:T(8,128)(2,1)}, bf16[512,2048]{1,0:T(8,128)(2,1)S(1)}, f32[16,32,128]{2,1,0:T(8,128)S(1)}, f32[32,128]{1,0:T(8,128)S(1)}, f32[1,128]{1,0:T(1,128)S(1)}) custom-call(f32[16,128]{1,0:T(8,128)S(1)} %broadcast_in_dim.14.inv_scale_ref, bf16[16,16,128]{2,1,0:T(8,128)(2,1)S(1)} %all-to-all-done.cols_ref, ...), custom_call_target="tpu_custom_call" | custom-call | tf_op jit(solution)/shard_map/tile/pallas_call | solution.py:154
  52.4 12.1 %all_to_all.36.received_ref = f32[16,32,128]{2,1,0:T(8,128)S(1)} all-to-all(f32[16,32,128]{2,1,0:T(8,128)S(1)} %get-tuple-element.18), channel_id=1, replica_groups=mesh['blk'=32,'team'=16] {'team'}, dimensions={0} | all-to-all | bytes 524288 | tf_op jit(solution)/shard_map/all_to_all | solution.py:187
  64.5 0.7 combine.1
  65.2 16.5 %all_to_all.37.v_ref = bf16[32,32,128]{2,1,0:T(8,128)(2,1)S(1)} all-to-all(bf16[32,32,128]{2,1,0:T(8,128)(2,1)S(1)} %get-tuple-element.21), channel_id=1, replica_groups=mesh['blk'=32,'team'=16] {'blk'}, dimensions={0} | all-to-all | bytes 524288 | tf_op jit(solution)/shard_map/all_to_all | solution.py:201
  81.8 6.4 %all-to-all-start.4 = ((bf16[16,32,128]{2,1,0:T(8,128)(2,1)}), bf16[16,32,128]{2,1,0:T(8,128)(2,1)S(1)}, u32[]{:S(2)}, u32[]{:S(2)}) async-start(bf16[16,32,128]{2,1,0:T(8,128)(2,1)} %get-tuple-element.22), calls=%async_computation.4 | async-start | bytes 262144 | tf_op jit(solution)/shard_map/all_to_all | solution.py:209
  88.2 5.8 %apply.1.partial_ref = f32[16,32,128]{2,1,0:T(8,128)S(1)} custom-call(bf16[3584,2048]{1,0:T(8,128)(2,1)} %get-tuple-element.16.tile_ref, bf16[512,2048]{1,0:T(8,128)(2,1)S(1)} %get-tuple-element.17.tail_ref, bf16[32,32,128]{2,1,0:T(8,128)(2,1)S(1)} %all_to_all.37.v_ref), custom_call_target="tpu_custom_call" | custom-call | flops 469762048 | bytes 14680064 | tf_op jit(solution)/shard_map/apply/pallas_call | solution.py:188
  94.0 0.4 all-to-all-done.4.cols_ref
  94.4 0.2 pack.1
  94.6 11.8 %all_to_all.38 = bf16[16,48,128]{2,1,0:T(8,128)(2,1)S(1)} all-to-all(bf16[16,48,128]{2,1,0:T(8,128)(2,1)S(1)} %pack.1), channel_id=1, replica_groups=mesh['blk'=32,'team'=16] {'team'}, dimensions={0} | all-to-all | bytes 393216 | tf_op jit(solution)/shard_map/all_to_all | solution.py:210
  106.5 15.8 %all_to_all.39 = f32[32,8,128]{2,1,0:T(8,128)S(1)} all-to-all(f32[32,8,128]{2,1,0:T(8,128)S(1)} %broadcast_in_dim.20), channel_id=1, replica_groups=mesh['blk'=32,'team'=16] {'blk'}, dimensions={0} | all-to-all | bytes 262144 | tf_op jit(solution)/shard_map/all_to_all | solution.py:143
  122.4 0.7 fusion.4
  (8 shorter events, 0.1 us)
Async XLA Ops:
  1.9 16.0 %all-to-all-start = ((bf16[16,16,128]{2,1,0:T(8,128)(2,1)}), bf16[16,16,128]{2,1,0:T(8,128)(2,1)S(1)}, u32[]{:S(2)}, u32[]{:S(2)}) async-start(bf16[16,16,128]{2,1,0:T(8,128)(2,1)} %broadcast_in_dim.17), calls=%async_computation | async-start | bytes 131072 | tf_op jit(solution)/shard_map/all_to_all | solution.py:143
  81.8 12.7 %all-to-all-start.4 = ((bf16[16,32,128]{2,1,0:T(8,128)(2,1)}), bf16[16,32,128]{2,1,0:T(8,128)(2,1)S(1)}, u32[]{:S(2)}, u32[]{:S(2)}) async-start(bf16[16,32,128]{2,1,0:T(8,128)(2,1)} %get-tuple-element.22), calls=%async_computation.4 | async-start | bytes 262144 | tf_op jit(solution)/shard_map/all_to_all | solution.py:209

commit v6 on v5

--- a/solution.py
+++ b/solution.py
@@ -39,17 +39,41 @@
     return pieces((-0.5 * LOG2E) * jnp.sum(scaled * scaled, axis=0, keepdims=True))
 
 
-def tile_kernel(
-    inv_scale_ref, cols_ref, rows_ref, field_ref, noise_ref,
-    tile_ref, tail_ref, partial_ref, field_out_ref, noise_out_ref,
-    lhs, rhs, held, sems, more_sems,
+def prepare_kernel(
+    points_ref, inv_scale_ref, noise_ref, weight_ref, field_ref,
+    to_team_ref, to_blk_ref, inv_scale_out_ref, noise_out_ref, weight_out_ref, field_out_ref,
+    points, inv_scale, weight, sems,
 ):
-    copies = [
-        pltpu.make_async_copy(field_ref, field_out_ref, more_sems.at[0]),
-        pltpu.make_async_copy(noise_ref, noise_out_ref, more_sems.at[1]),
+    pairs = [
+        (points_ref, points),
+        (field_ref, field_out_ref),
+        (inv_scale_ref, inv_scale),
+        (weight_ref, weight),
+        (noise_ref, noise_out_ref),
     ]
+    copies = [pltpu.make_async_copy(source, target, sems.at[i]) for i, (source, target) in enumerate(pairs)]
     for copy in copies:
         copy.start()
+    for copy in copies:
+        copy.wait()
+    own = points[...]
+    for m in range(to_team_ref.shape[0]):
+        to_team_ref[m] = own
+    lowered = field_out_ref[...].astype(bf16)
+    for m in range(to_blk_ref.shape[0]):
+        to_blk_ref[m, :DIMS, :] = own
+        to_blk_ref[m, DIMS:, :] = lowered
+    row = lax.broadcasted_iota(jnp.int32, (DIMS, DIMS), 0)
+    lane = lax.broadcasted_iota(jnp.int32, (DIMS, DIMS), 1)
+    spread = jnp.where(row == lane, jnp.broadcast_to(inv_scale[...], (DIMS, DIMS)), 0.0)
+    inv_scale_out_ref[...] = jnp.broadcast_to(jnp.sum(spread, axis=1, keepdims=True), (DIMS, LANES))
+    weight_out_ref[...] = jnp.broadcast_to(weight[...], (1, LANES))
+
+
+def tile_kernel(
+    inv_scale_ref, cols_ref, rows_ref, tile_ref, tail_ref, partial_ref, lhs, rhs, held, sems
+):
+    copies = []
     inv_scale = inv_scale_ref[...]
     n_cols, n_rows = cols_ref.shape[0], rows_ref.shape[0]
     deep = tail_ref.shape[0]
@@ -123,11 +147,13 @@
         inner = inner + cols_ref[m].astype(f32) * partial_ref[m]
     inner = weight_ref[...] * inner + noise_ref[...] * applied * applied
     lane = lax.broadcasted_iota(jnp.int32, (PROBES, LANES), 1)
-    sums = jnp.zeros((PROBES, LANES), f32)
-    for place, product in enumerate((targets * targets, targets * applied, applied * applied, inner)):
-        for piece, part in enumerate(pieces(jnp.sum(product, axis=1, keepdims=True))):
-            sums = jnp.where(lane == 4 * piece + place, part, sums)
-    sums = jnp.concatenate([sums, jnp.zeros((LANES - PROBES, LANES), f32)], axis=0).T[:EXTRA].astype(bf16)
+    groups = []
+    for product in (targets * targets, targets * applied, applied * applied, inner):
+        group = jnp.zeros((PROBES, LANES), f32)
+        for place, part in enumerate(pieces(jnp.sum(product, axis=1, keepdims=True))):
+            group = jnp.where(lane == place, part, group)
+        groups.append(group)
+    sums = jnp.concatenate(groups, axis=0).T[:EXTRA].astype(bf16)
     for m in range(partial_ref.shape[0]):
         message_ref[m, PROBES:, :] = sums
 
@@ -139,39 +165,50 @@
 def shards(points, inv_scale, noise_var, signal_var, targets):
     blks, teams = lax.axis_size("blk"), lax.axis_size("team")
 
-    def to_all(x, axis, size):
-        return lax.all_to_all(jnp.broadcast_to(x[None], (size, *x.shape)), axis, 0, 0)
-
-    cols = to_all(points, "team", teams)
-    own = jnp.concatenate([points, targets.astype(bf16)], axis=0)
-    own, inv_scale, weight = lax.optimization_barrier(
-        (own, jnp.broadcast_to(inv_scale[:, None], (DIMS, LANES)), jnp.broadcast_to(signal_var[None], (1, LANES)))
-    )
-    rows = to_all(own, "blk", blks)
+    to_team, to_blk, inv_scale, noise, weight, field = pl.pallas_call(
+        prepare_kernel,
+        out_shape=(
+            jax.ShapeDtypeStruct((teams, DIMS, LANES), bf16),
+            jax.ShapeDtypeStruct((blks, DIMS + PROBES, LANES), bf16),
+            jax.ShapeDtypeStruct((DIMS, LANES), f32),
+            jax.ShapeDtypeStruct((1, LANES), f32),
+            jax.ShapeDtypeStruct((1, LANES), f32),
+            jax.ShapeDtypeStruct((PROBES, LANES), f32),
+        ),
+        in_specs=[pl.BlockSpec(memory_space=pl.ANY)] * 5,
+        out_specs=[VMEM] * 6,
+        scratch_shapes=[
+            pltpu.VMEM((DIMS, LANES), bf16),
+            pltpu.VMEM((1, DIMS), f32),
+            pltpu.VMEM((1, 1), f32),
+            pltpu.SemaphoreType.DMA((5,)),
+        ],
+        compiler_params=SMALL,
+        name="prepare",
+    )(in_hbm(points), in_hbm(inv_scale[None]), in_hbm(noise_var[None]), signal_var[None], in_hbm(targets))
+    cols = lax.all_to_all(to_team, "team", 0, 0)
+    rows = lax.all_to_all(to_blk, "blk", 0, 0)
     deep, wide = 512, teams * LANES
     tile_shape = (blks * LANES - deep, wide)
     sems = pltpu.SemaphoreType.DMA((tile_shape[0] // deep,))
-    tile, tail, partial, field, noise = pl.pallas_call(
+    tile, tail, partial = pl.pallas_call(
         tile_kernel,
         out_shape=(
             pltpu.HBM(tile_shape, bf16),
             jax.ShapeDtypeStruct((deep, wide), bf16),
             jax.ShapeDtypeStruct((teams, PROBES, LANES), f32),
-            jax.ShapeDtypeStruct((PROBES, LANES), f32),
-            jax.ShapeDtypeStruct((1, LANES), f32),
-        ),
-        in_specs=[VMEM] * 3 + [HBM] * 2,
-        out_specs=[HBM] + [VMEM] * 4,
+        ),
+        in_specs=[VMEM] * 3,
+        out_specs=[HBM] + [VMEM] * 2,
         scratch_shapes=[
             pltpu.VMEM((blks * LANES, FEATURES), bf16),
             pltpu.VMEM((FEATURES, wide), bf16),
             pltpu.VMEM(tile_shape, bf16),
             sems,
-            pltpu.SemaphoreType.DMA((2,)),
         ],
         compiler_params=LARGE,
         name="tile",
-    )(inv_scale, cols, rows, in_hbm(targets), in_hbm(noise_var[None, :]))
+    )(inv_scale, cols, rows)
 
     applied, to_blk, to_team = pl.pallas_call(
         combine_kernel,
@@ -210,9 +247,10 @@
     total = jnp.sum(lax.all_to_all(message, "team", 0, 0).astype(f32), axis=0)
     twice = noise * applied + weight * total[:PROBES]
 
-    sums = total[PROBES : PROBES + 8] + total[PROBES + 8 :]
-    sums = jnp.sum(to_all(sums, "blk", blks), axis=0)
-    tt, ta, aa, ab = [(sums[i] + sums[i + 4])[:PROBES, None] for i in range(4)]
+    sums = jnp.sum(total[PROBES:], axis=0, keepdims=True)
+    sums = jnp.broadcast_to(sums[None], (blks, 1, LANES))
+    sums = jnp.sum(lax.all_to_all(sums, "blk", 0, 0), axis=(0, 1))
+    tt, ta, aa, ab = [sums[i * PROBES : (i + 1) * PROBES, None] for i in range(4)]
     step_0 = tt / ta
     norm_1 = tt - 2.0 * step_0 * ta + step_0 * step_0 * aa
     ratio = norm_1 / tt

time: 124 us -> 123 us (level)
  blocking collectives: 82.9 us -> 98.4 us
  starting transfers between devices: 16.6 us -> 6.43 us
  waiting for transfers between devices: 3.53 us -> 0.43 us
  local copies, waits for them, and re-layouts: 2.1 us -> 0.01 us
  other arithmetic: 2.22 us -> 0.94 us
    all_to_all x2 -> x3, blocking collectives: 42.4 us -> 57.9 us  [the longest x1 27.3 us: shards(): rows = lax.all_to_all(to_blk, 'blk', 0, 0)]
    all_to_all x1 -> x0, starting transfers between devices: 10.2 us -> none  [to_all(): lax.all_to_all(jnp.broadcast_to(x[None], (size, *x.shape)), axis, 0, 0)]
    all_to_all x1 -> x0, waiting for transfers between devices: 3.1 us -> none  [to_all(): lax.all_to_all(jnp.broadcast_to(x[None], (size, *x.shape)), axis, 0, 0)]
    broadcast_in_dim x5 -> x1, local copies, waits for them, and re-layouts: 2.1 us -> 0.01 us  [shards(): sums = jnp.broadcast_to(sums[None], (blks, 1, LANES))]
  transfers between devices with their start and end apart: 2 -> 1, of which waited for: 2 -> 1; matrix products, arithmetic and copies ran while one was open for 2% -> 0% of each run, Pallas kernels for 5% -> 5%
where the time goes in v6:
time: 123 us
  blocking collectives  98.4 us (80%)
  Pallas kernels  15.2 us (12%)
  starting transfers between devices  6.43 us (5%)
  between operations  1.31 us (1%)
    all_to_all x1, blocking collectives, shards(): rows = lax.all_to_all(to_blk, 'blk', 0, 0)  27.3 us
    all_to_all x1, blocking collectives, shards(): lax.all_to_all(to_blk, 'blk', 0, 0)  16.5 us
    all_to_all x1, blocking collectives, shards(): sums = jnp.sum(lax.all_to_all(sums, 'blk', 0, 0), axis=(0, 1))  15.4 us
    all_to_all x1, blocking collectives, shards(): cols = lax.all_to_all(to_team, 'team', 0, 0)  15.2 us
    all_to_all x1, blocking collectives, shards(): lax.all_to_all(partial, 'team', 0, 0)  12.1 us
    all_to_all x1, blocking collectives, shards(): total = jnp.sum(lax.all_to_all(message, 'team', 0, 0).astype(f32), axis=0)  11.8 us
    pallas_call x1, Pallas kernels, shards(): pl.pallas_call(tile_kernel, out_shape=(pltpu.HBM(tile_shape, bf16), jax.S...  7.69 us
    all_to_all x1, starting transfers between devices, shards(): lax.all_to_all(to_team, 'team', 0, 0)  6.43 us
  transfers between devices with their start and end apart: 1, of which 1 were waited for; matrix products, arithmetic and copies ran while one was open for 0% of the time, Pallas kernels for 5%

profile of v6, /device:TPU:1, one launch (start us, length us, event | category | flops | bytes accessed | tf_op | source)
XLA Modules:
  0.0 122.7 jit_solution(6513686730540601690)
XLA Ops:
  1.3 0.9 prepare.1
  2.2 15.2 %all_to_all.35.cols_ref = bf16[16,16,128]{2,1,0:T(8,128)(2,1)S(1)} all-to-all(bf16[16,16,128]{2,1,0:T(8,128)(2,1)S(1)} %get-tuple-element.16), channel_id=1, replica_groups=mesh['blk'=32,'team'=16] {'team'}, dimensions={0} | all-to-all | bytes 131072 | tf_op jit(solution)/shard_map/all_to_all | solution.py:189
  17.3 27.3 %all_to_all.36.rows_ref = bf16[32,48,128]{2,1,0:T(8,128)(2,1)S(1)} all-to-all(bf16[32,48,128]{2,1,0:T(8,128)(2,1)S(1)} %get-tuple-element.17), channel_id=1, replica_groups=mesh['blk'=32,'team'=16] {'blk'}, dimensions={0} | all-to-all | bytes 786432 | tf_op jit(solution)/shard_map/all_to_all | solution.py:190
  44.7 7.7 %tile.1 = (bf16[3584,2048]{1,0:T(8,128)(2,1)}, bf16[512,2048]{1,0:T(8,128)(2,1)S(1)}, f32[16,32,128]{2,1,0:T(8,128)S(1)}) custom-call(f32[16,128]{1,0:T(8,128)S(1)} %get-tuple-element.15.inv_scale_ref, bf16[16,16,128]{2,1,0:T(8,128)(2,1)S(1)} %all_to_all.35.cols_ref, bf16[32,48,128]{2,1,0:T(8,128)(2,1)S(1)} %all_to_all.36.rows_ref), custom_call_target="tpu_custom_call" | custom-call | tf_op jit(solution)/shard_map/tile/pallas_call | solution.py:194
  52.4 12.1 %all_to_all.37.received_ref = f32[16,32,128]{2,1,0:T(8,128)S(1)} all-to-all(f32[16,32,128]{2,1,0:T(8,128)S(1)} %get-tuple-element.20), channel_id=1, replica_groups=mesh['blk'=32,'team'=16] {'team'}, dimensions={0} | all-to-all | bytes 524288 | tf_op jit(solution)/shard_map/all_to_all | solution.py:224
  64.5 0.7 combine.1
  65.2 16.5 %all_to_all.38.v_ref = bf16[32,32,128]{2,1,0:T(8,128)(2,1)S(1)} all-to-all(bf16[32,32,128]{2,1,0:T(8,128)(2,1)S(1)} %get-tuple-element.23), channel_id=1, replica_groups=mesh['blk'=32,'team'=16] {'blk'}, dimensions={0} | all-to-all | bytes 524288 | tf_op jit(solution)/shard_map/all_to_all | solution.py:238
  81.7 6.4 %all-to-all-start.4 = ((bf16[16,32,128]{2,1,0:T(8,128)(2,1)}), bf16[16,32,128]{2,1,0:T(8,128)(2,1)S(1)}, u32[]{:S(2)}, u32[]{:S(2)}) async-start(bf16[16,32,128]{2,1,0:T(8,128)(2,1)} %get-tuple-element.24), calls=%async_computation.4 | async-start | bytes 262144 | tf_op jit(solution)/shard_map/all_to_all | solution.py:246
  88.1 5.8 %apply.1.partial_ref = f32[16,32,128]{2,1,0:T(8,128)S(1)} custom-call(bf16[3584,2048]{1,0:T(8,128)(2,1)} %get-tuple-element.18.tile_ref, bf16[512,2048]{1,0:T(8,128)(2,1)S(1)} %get-tuple-element.19.tail_ref, bf16[32,32,128]{2,1,0:T(8,128)(2,1)S(1)} %all_to_all.38.v_ref), custom_call_target="tpu_custom_call" | custom-call | flops 469762048 | bytes 14680064 | tf_op jit(solution)/shard_map/apply/pallas_call | solution.py:225
  93.9 0.4 all-to-all-done.4.cols_ref
  94.4 0.2 pack.1
  94.5 11.8 %all_to_all.39 = bf16[16,48,128]{2,1,0:T(8,128)(2,1)S(1)} all-to-all(bf16[16,48,128]{2,1,0:T(8,128)(2,1)S(1)} %pack.1), channel_id=1, replica_groups=mesh['blk'=32,'team'=16] {'team'}, dimensions={0} | all-to-all | bytes 393216 | tf_op jit(solution)/shard_map/all_to_all | solution.py:247
  106.4 15.4 %all_to_all.40 = f32[32,1,128]{2,1,0:T(1,128)S(1)} all-to-all(f32[32,1,128]{2,1,0:T(1,128)S(1)} %broadcast_in_dim.21), channel_id=1, replica_groups=mesh['blk'=32,'team'=16] {'blk'}, dimensions={0} | all-to-all | bytes 32768 | tf_op jit(solution)/shard_map/all_to_all | solution.py:252
  121.8 0.1 broadcast_add_fusion
  121.9 0.1 add_divide_fusion
  122.0 0.7 fusion.4
  (4 shorter events, 0.1 us)
Async XLA Ops:
  81.7 12.7 %all-to-all-start.4 = ((bf16[16,32,128]{2,1,0:T(8,128)(2,1)}), bf16[16,32,128]{2,1,0:T(8,128)(2,1)S(1)}, u32[]{:S(2)}, u32[]{:S(2)}) async-start(bf16[16,32,128]{2,1,0:T(8,128)(2,1)} %get-tuple-element.24), calls=%async_computation.4 | async-start | bytes 262144 | tf_op jit(solution)/shard_map/all_to_all | solution.py:246

commit v7 on v6

--- a/solution.py
+++ b/solution.py
@@ -139,12 +139,15 @@
         partial_ref[m] = total[:, m * LANES : (m + 1) * LANES]
 
 
-def pack_kernel(weight_ref, partial_ref, cols_ref, targets_ref, applied_ref, noise_ref, message_ref):
+def pack_kernel(weight_ref, partial_ref, cols_ref, targets_ref, applied_ref, noise_ref, message_ref, own_ref):
+    here = lax.axis_index("team")
     targets, applied = targets_ref[...], applied_ref[...]
     inner = jnp.zeros(targets.shape, f32)
     for m in range(partial_ref.shape[0]):
         message_ref[m, :PROBES, :] = partial_ref[m].astype(bf16)
         inner = inner + cols_ref[m].astype(f32) * partial_ref[m]
+    own_ref[...] = partial_ref[here]
+    message_ref[here, :PROBES, :] = jnp.zeros((PROBES, LANES), bf16)
     inner = weight_ref[...] * inner + noise_ref[...] * applied * applied
     lane = lax.broadcasted_iota(jnp.int32, (PROBES, LANES), 1)
     groups = []
@@ -156,6 +159,10 @@
     sums = jnp.concatenate(groups, axis=0).T[:EXTRA].astype(bf16)
     for m in range(partial_ref.shape[0]):
         message_ref[m, PROBES:, :] = sums
+
+
+def rounded(x):
+    return lax.reduce_precision(x, 8, 7)
 
 
 def in_hbm(x):
@@ -217,7 +224,7 @@
             jax.ShapeDtypeStruct((blks, PROBES, LANES), bf16),
             jax.ShapeDtypeStruct((teams, PROBES, LANES), bf16),
         ),
-        in_specs=[VMEM] + [VMEM] * 3,
+        in_specs=[VMEM] * 4,
         out_specs=[VMEM] * 3,
         compiler_params=SMALL,
         name="combine",
@@ -236,16 +243,19 @@
         ),
         name="apply",
     )(in_hbm(tile), tail, lax.all_to_all(to_blk, "blk", 0, 0))
-    message = pl.pallas_call(
+    message, own = pl.pallas_call(
         pack_kernel,
-        out_shape=jax.ShapeDtypeStruct((teams, PROBES + EXTRA, LANES), bf16),
-        in_specs=[VMEM] + [VMEM] * 5,
-        out_specs=VMEM,
+        out_shape=(
+            jax.ShapeDtypeStruct((teams, PROBES + EXTRA, LANES), bf16),
+            jax.ShapeDtypeStruct((PROBES, LANES), f32),
+        ),
+        in_specs=[VMEM] * 6,
+        out_specs=[VMEM] * 2,
         compiler_params=SMALL,
         name="pack",
     )(weight, partial, lax.all_to_all(to_team, "team", 0, 0), field, applied, noise)
     total = jnp.sum(lax.all_to_all(message, "team", 0, 0).astype(f32), axis=0)
-    twice = noise * applied + weight * total[:PROBES]
+    twice = noise * applied + weight * (total[:PROBES] + own)
 
     sums = jnp.sum(total[PROBES:], axis=0, keepdims=True)
     sums = jnp.broadcast_to(sums[None], (blks, 1, LANES))
@@ -258,7 +268,8 @@
     step_1 = norm_1 / curvature
     residual = field - step_0 * applied
     direction = residual + ratio * field
-    slope = (1 + ratio) * applied - step_0 * twice
+    exact = (1 + ratio) * rounded(field) - step_0 * rounded(applied)
+    slope = (1 + ratio) * applied - step_0 * twice + weight * (rounded(direction) - exact)
     return step_0 * field + step_1 * direction, residual - step_1 * slope
 
 

time: 123 us -> 123 us (level)
  no operation moved by 1% of the time
where the time goes in v7:
time: 123 us
  blocking collectives  98.4 us (80%)
  Pallas kernels  15.2 us (12%)
  starting transfers between devices  6.43 us (5%)
  between operations  1.31 us (1%)
    all_to_all x1, blocking collectives, shards(): rows = lax.all_to_all(to_blk, 'blk', 0, 0)  27.3 us
    all_to_all x1, blocking collectives, shards(): lax.all_to_all(to_blk, 'blk', 0, 0)  16.5 us
    all_to_all x1, blocking collectives, shards(): sums = jnp.sum(lax.all_to_all(sums, 'blk', 0, 0), axis=(0, 1))  15.4 us
    all_to_all x1, blocking collectives, shards(): cols = lax.all_to_all(to_team, 'team', 0, 0)  15.2 us
    all_to_all x1, blocking collectives, shards(): lax.all_to_all(partial, 'team', 0, 0)  12.1 us
    all_to_all x1, blocking collectives, shards(): total = jnp.sum(lax.all_to_all(message, 'team', 0, 0).astype(f32), axis=0)  11.8 us
    pallas_call x1, Pallas kernels, shards(): pl.pallas_call(tile_kernel, out_shape=(pltpu.HBM(tile_shape, bf16), jax.S...  7.69 us
    all_to_all x1, starting transfers between devices, shards(): lax.all_to_all(to_team, 'team', 0, 0)  6.43 us
  transfers between devices with their start and end apart: 1, of which 1 were waited for; matrix products, arithmetic and copies ran while one was open for 0% of the time, Pallas kernels for 5%

profile of v7, /device:TPU:1, one launch (start us, length us, event | category | flops | bytes accessed | tf_op | source)
XLA Modules:
  0.0 122.7 jit_solution(2407324172679633420)
XLA Ops:
  1.3 0.9 prepare.1
  2.2 15.2 %all_to_all.35.cols_ref = bf16[16,16,128]{2,1,0:T(8,128)(2,1)S(1)} all-to-all(bf16[16,16,128]{2,1,0:T(8,128)(2,1)S(1)} %get-tuple-element.18), channel_id=1, replica_groups=mesh['blk'=32,'team'=16] {'team'}, dimensions={0} | all-to-all | bytes 131072 | tf_op jit(solution)/shard_map/all_to_all | solution.py:196
  17.3 27.3 %all_to_all.36.rows_ref = bf16[32,48,128]{2,1,0:T(8,128)(2,1)S(1)} all-to-all(bf16[32,48,128]{2,1,0:T(8,128)(2,1)S(1)} %get-tuple-element.19), channel_id=1, replica_groups=mesh['blk'=32,'team'=16] {'blk'}, dimensions={0} | all-to-all | bytes 786432 | tf_op jit(solution)/shard_map/all_to_all | solution.py:197
  44.7 7.7 %tile.1 = (bf16[3584,2048]{1,0:T(8,128)(2,1)}, bf16[512,2048]{1,0:T(8,128)(2,1)S(1)}, f32[16,32,128]{2,1,0:T(8,128)S(1)}) custom-call(f32[16,128]{1,0:T(8,128)S(1)} %get-tuple-element.17.inv_scale_ref, bf16[16,16,128]{2,1,0:T(8,128)(2,1)S(1)} %all_to_all.35.cols_ref, bf16[32,48,128]{2,1,0:T(8,128)(2,1)S(1)} %all_to_all.36.rows_ref), custom_call_target="tpu_custom_call" | custom-call | tf_op jit(solution)/shard_map/tile/pallas_call | solution.py:201
  52.4 12.1 %all_to_all.37.received_ref = f32[16,32,128]{2,1,0:T(8,128)S(1)} all-to-all(f32[16,32,128]{2,1,0:T(8,128)S(1)} %get-tuple-element.22), channel_id=1, replica_groups=mesh['blk'=32,'team'=16] {'team'}, dimensions={0} | all-to-all | bytes 524288 | tf_op jit(solution)/shard_map/all_to_all | solution.py:231
  64.5 0.7 combine.1
  65.2 16.5 %all_to_all.38.v_ref = bf16[32,32,128]{2,1,0:T(8,128)(2,1)S(1)} all-to-all(bf16[32,32,128]{2,1,0:T(8,128)(2,1)S(1)} %get-tuple-element.25), channel_id=1, replica_groups=mesh['blk'=32,'team'=16] {'blk'}, dimensions={0} | all-to-all | bytes 524288 | tf_op jit(solution)/shard_map/all_to_all | solution.py:245
  81.7 6.4 %all-to-all-start.4 = ((bf16[16,32,128]{2,1,0:T(8,128)(2,1)}), bf16[16,32,128]{2,1,0:T(8,128)(2,1)S(1)}, u32[]{:S(2)}, u32[]{:S(2)}) async-start(bf16[16,32,128]{2,1,0:T(8,128)(2,1)} %get-tuple-element.26), calls=%async_computation.4 | async-start | bytes 262144 | tf_op jit(solution)/shard_map/all_to_all | solution.py:256
  88.1 5.8 %apply.1.partial_ref = f32[16,32,128]{2,1,0:T(8,128)S(1)} custom-call(bf16[3584,2048]{1,0:T(8,128)(2,1)} %get-tuple-element.20.tile_ref, bf16[512,2048]{1,0:T(8,128)(2,1)S(1)} %get-tuple-element.21.tail_ref, bf16[32,32,128]{2,1,0:T(8,128)(2,1)S(1)} %all_to_all.38.v_ref), custom_call_target="tpu_custom_call" | custom-call | flops 469762048 | bytes 14680064 | tf_op jit(solution)/shard_map/apply/pallas_call | solution.py:232
  93.9 0.4 all-to-all-done.4.cols_ref
  94.4 0.2 pack.1
  94.5 11.8 %all_to_all.39 = bf16[16,48,128]{2,1,0:T(8,128)(2,1)S(1)} all-to-all(bf16[16,48,128]{2,1,0:T(8,128)(2,1)S(1)} %get-tuple-element.28), channel_id=1, replica_groups=mesh['blk'=32,'team'=16] {'team'}, dimensions={0} | all-to-all | bytes 393216 | tf_op jit(solution)/shard_map/all_to_all | solution.py:257
  106.4 15.4 %all_to_all.40 = f32[32,1,128]{2,1,0:T(1,128)S(1)} all-to-all(f32[32,1,128]{2,1,0:T(1,128)S(1)} %broadcast_in_dim.21), channel_id=1, replica_groups=mesh['blk'=32,'team'=16] {'blk'}, dimensions={0} | all-to-all | bytes 32768 | tf_op jit(solution)/shard_map/all_to_all | solution.py:262
  121.8 0.1 broadcast_add_fusion
  121.9 0.1 add_divide_fusion
  122.0 0.7 fusion.6
  (4 shorter events, 0.1 us)
Async XLA Ops:
  81.7 12.7 %all-to-all-start.4 = ((bf16[16,32,128]{2,1,0:T(8,128)(2,1)}), bf16[16,32,128]{2,1,0:T(8,128)(2,1)S(1)}, u32[]{:S(2)}, u32[]{:S(2)}) async-start(bf16[16,32,128]{2,1,0:T(8,128)(2,1)} %get-tuple-element.26), calls=%async_computation.4 | async-start | bytes 262144 | tf_op jit(solution)/shard_map/all_to_all | solution.py:256

commit v8 on v7

--- a/solution.py
+++ b/solution.py
@@ -11,6 +11,7 @@
 DIMS, PROBES, LANES = 16, 32, 128
 FEATURES = 4 * DIMS
 EXTRA = 16
+TINY = 1e-20
 LOG2E = math.log2(math.e)
 VMEM = pl.BlockSpec(memory_space=pltpu.VMEM)
 HBM = pl.BlockSpec(memory_space=pltpu.HBM)
@@ -107,16 +108,26 @@
         copy.wait()
 
 
-def combine_kernel(weight_ref, received_ref, field_ref, noise_ref, applied_ref, to_blk_ref, to_team_ref):
+def combine_kernel(
+    weight_ref, received_ref, field_ref, noise_ref, product_ref, applied_ref, sent_ref, to_blk_ref, to_team_ref
+):
     total = received_ref[0]
     for m in range(1, received_ref.shape[0]):
         total = total + received_ref[m]
-    applied = noise_ref[...] * field_ref[...] + weight_ref[...] * total
+    product_ref[...] = total
+    field = field_ref[...]
+    applied = noise_ref[...] * field + weight_ref[...] * total
     applied_ref[...] = applied
-    lowered = applied.astype(bf16)
+    ff, fa, aa = [jnp.sum(x, axis=1, keepdims=True) for x in (field * field, field * applied, applied * applied)]
+    multiple = jnp.minimum(aa / jnp.maximum(fa, TINY), 4.0 * jnp.sqrt(aa / jnp.maximum(ff, TINY)))
+    sent = applied - multiple * (field - field.astype(bf16).astype(f32))
+    high = sent.astype(bf16)
+    low = (sent - high.astype(f32)).astype(bf16)
+    sent_ref[...] = high.astype(f32) + low.astype(f32)
     for copies_ref in (to_blk_ref, to_team_ref):
         for m in range(copies_ref.shape[0]):
-            copies_ref[m] = lowered
+            copies_ref[m, :PROBES, :] = high
+            copies_ref[m, PROBES:, :] = low
 
 
 def apply_kernel(tile_ref, tail_ref, v_ref, partial_ref, held, sems):
@@ -135,27 +146,39 @@
     for start, copy in copies:
         copy.wait()
         total = total + product(start, held[start : start + deep, :])
+    total = total[:PROBES] + total[PROBES:]
     for m in range(partial_ref.shape[0]):
         partial_ref[m] = total[:, m * LANES : (m + 1) * LANES]
 
 
-def pack_kernel(weight_ref, partial_ref, cols_ref, targets_ref, applied_ref, noise_ref, message_ref, own_ref):
+def pack_kernel(
+    weight_ref, partial_ref, cols_ref, field_ref, noise_ref, product_ref, applied_ref, sent_ref, message_ref, own_ref
+):
     here = lax.axis_index("team")
-    targets, applied = targets_ref[...], applied_ref[...]
-    inner = jnp.zeros(targets.shape, f32)
+    weight, noise = weight_ref[...], noise_ref[...]
+    field, applied, product = field_ref[...], applied_ref[...], product_ref[...]
+    inner = jnp.zeros(field.shape, f32)
     for m in range(partial_ref.shape[0]):
         message_ref[m, :PROBES, :] = partial_ref[m].astype(bf16)
-        inner = inner + cols_ref[m].astype(f32) * partial_ref[m]
+        sent = cols_ref[m, :PROBES, :].astype(f32) + cols_ref[m, PROBES:, :].astype(f32)
+        inner = inner + sent * partial_ref[m]
     own_ref[...] = partial_ref[here]
     message_ref[here, :PROBES, :] = jnp.zeros((PROBES, LANES), bf16)
-    inner = weight_ref[...] * inner + noise_ref[...] * applied * applied
     lane = lax.broadcasted_iota(jnp.int32, (PROBES, LANES), 1)
-    groups = []
-    for product in (targets * targets, targets * applied, applied * applied, inner):
-        group = jnp.zeros((PROBES, LANES), f32)
-        for place, part in enumerate(pieces(jnp.sum(product, axis=1, keepdims=True))):
-            group = jnp.where(lane == place, part, group)
-        groups.append(group)
+
+    def group(values, first):
+        block = jnp.zeros((PROBES, LANES), f32)
+        for place, part in enumerate(pieces(jnp.sum(values, axis=1, keepdims=True))):
+            block = jnp.where(lane == first + place, part, block)
+        return block
+
+    lowered = field.astype(bf16).astype(f32)
+    groups = [
+        group(field * field, 0) + group(noise * field * applied + weight * sent_ref[...] * product, 8),
+        group(field * applied, 0) + group(noise * applied * applied + weight * inner, 8),
+        group(applied * applied, 0),
+        group(noise * field * field + weight * lowered * product, 0),
+    ]
     sums = jnp.concatenate(groups, axis=0).T[:EXTRA].astype(bf16)
     for m in range(partial_ref.shape[0]):
         message_ref[m, PROBES:, :] = sums
@@ -217,15 +240,18 @@
         name="tile",
     )(inv_scale, cols, rows)
 
-    applied, to_blk, to_team = pl.pallas_call(
+    block = jax.ShapeDtypeStruct((PROBES, LANES), f32)
+    product, applied, sent, to_blk, to_team = pl.pallas_call(
         combine_kernel,
         out_shape=(
-            jax.ShapeDtypeStruct((PROBES, LANES), f32),
-            jax.ShapeDtypeStruct((blks, PROBES, LANES), bf16),
-            jax.ShapeDtypeStruct((teams, PROBES, LANES), bf16),
+            block,
+            block,
+            block,
+            jax.ShapeDtypeStruct((blks, 2 * PROBES, LANES), bf16),
+            jax.ShapeDtypeStruct((teams, 2 * PROBES, LANES), bf16),
         ),
         in_specs=[VMEM] * 4,
-        out_specs=[VMEM] * 3,
+        out_specs=[VMEM] * 5,
         compiler_params=SMALL,
         name="combine",
     )(weight, lax.all_to_all(partial, "team", 0, 0), field, noise)
@@ -247,28 +273,29 @@
         pack_kernel,
         out_shape=(
             jax.ShapeDtypeStruct((teams, PROBES + EXTRA, LANES), bf16),
-            jax.ShapeDtypeStruct((PROBES, LANES), f32),
-        ),
-        in_specs=[VMEM] * 6,
+            block,
+        ),
+        in_specs=[VMEM] * 8,
         out_specs=[VMEM] * 2,
         compiler_params=SMALL,
         name="pack",
-    )(weight, partial, lax.all_to_all(to_team, "team", 0, 0), field, applied, noise)
+    )(weight, partial, lax.all_to_all(to_team, "team", 0, 0), field, noise, product, applied, sent)
     total = jnp.sum(lax.all_to_all(message, "team", 0, 0).astype(f32), axis=0)
     twice = noise * applied + weight * (total[:PROBES] + own)
 
-    sums = jnp.sum(total[PROBES:], axis=0, keepdims=True)
-    sums = jnp.broadcast_to(sums[None], (blks, 1, LANES))
-    sums = jnp.sum(lax.all_to_all(sums, "blk", 0, 0), axis=(0, 1))
-    tt, ta, aa, ab = [sums[i * PROBES : (i + 1) * PROBES, None] for i in range(4)]
+    sums = jnp.sum(total[PROBES:].reshape(2, EXTRA // 2, LANES), axis=1)
+    sums = jnp.broadcast_to(sums[None], (blks, 2, LANES))
+    sums = jnp.sum(lax.all_to_all(sums, "blk", 0, 0), axis=0)
+    tt, ta, aa, c0 = [sums[0, i * PROBES : (i + 1) * PROBES, None] for i in range(4)]
+    c1, c2 = [sums[1, i * PROBES : (i + 1) * PROBES, None] for i in range(2)]
     step_0 = tt / ta
     norm_1 = tt - 2.0 * step_0 * ta + step_0 * step_0 * aa
     ratio = norm_1 / tt
-    curvature = (1 + ratio) * (1 + ratio) * ta - 2.0 * (1 + ratio) * step_0 * aa + step_0 * step_0 * ab
+    curvature = (1 + ratio) * (1 + ratio) * c0 - 2.0 * (1 + ratio) * step_0 * c1 + step_0 * step_0 * c2
     step_1 = norm_1 / curvature
     residual = field - step_0 * applied
     direction = residual + ratio * field
-    exact = (1 + ratio) * rounded(field) - step_0 * rounded(applied)
+    exact = (1 + ratio) * rounded(field) - step_0 * sent
     slope = (1 + ratio) * applied - step_0 * twice + weight * (rounded(direction) - exact)
     return step_0 * field + step_1 * direction, residual - step_1 * slope
 

time: 123 us -> 129 us (1.049)
  blocking collectives: 98.4 us -> 103 us
    all_to_all x1, blocking collectives: 16.5 us -> 21.4 us  [shards(): lax.all_to_all(to_blk, 'blk', 0, 0)]
where the time goes in v8:
time: 129 us
  blocking collectives  103 us (80%)
  Pallas kernels  15.5 us (12%)
  starting transfers between devices  6.56 us (5%)
  waiting for transfers between devices  1.43 us (1%)
  between operations  1.31 us (1%)
    all_to_all x1, blocking collectives, shards(): rows = lax.all_to_all(to_blk, 'blk', 0, 0)  27.3 us
    all_to_all x1, blocking collectives, shards(): lax.all_to_all(to_blk, 'blk', 0, 0)  21.4 us
    all_to_all x1, blocking collectives, shards(): sums = jnp.sum(lax.all_to_all(sums, 'blk', 0, 0), axis=0)  16.2 us
    all_to_all x1, blocking collectives, shards(): cols = lax.all_to_all(to_team, 'team', 0, 0)  15.2 us
    all_to_all x1, blocking collectives, shards(): lax.all_to_all(partial, 'team', 0, 0)  12.1 us
    all_to_all x1, blocking collectives, shards(): total = jnp.sum(lax.all_to_all(message, 'team', 0, 0).astype(f32), axis=0)  10.9 us
    pallas_call x1, Pallas kernels, shards(): pl.pallas_call(tile_kernel, out_shape=(pltpu.HBM(tile_shape, bf16), jax.S...  7.69 us
    all_to_all x1, starting transfers between devices, shards(): lax.all_to_all(to_team, 'team', 0, 0)  6.56 us
  transfers between devices with their start and end apart: 1, of which 1 were waited for; matrix products, arithmetic and copies ran while one was open for 0% of the time, Pallas kernels for 5%

profile of v8, /device:TPU:1, one launch (start us, length us, event | category | flops | bytes accessed | tf_op | source)
XLA Modules:
  0.0 128.8 jit_solution(1669733324618178697)
XLA Ops:
  1.3 0.9 prepare.1
  2.2 15.2 %all_to_all.35.cols_ref = bf16[16,16,128]{2,1,0:T(8,128)(2,1)S(1)} all-to-all(bf16[16,16,128]{2,1,0:T(8,128)(2,1)S(1)} %get-tuple-element.20), channel_id=1, replica_groups=mesh['blk'=32,'team'=16] {'team'}, dimensions={0} | all-to-all | bytes 131072 | tf_op jit(solution)/shard_map/all_to_all | solution.py:219
  17.3 27.3 %all_to_all.36.rows_ref = bf16[32,48,128]{2,1,0:T(8,128)(2,1)S(1)} all-to-all(bf16[32,48,128]{2,1,0:T(8,128)(2,1)S(1)} %get-tuple-element.21), channel_id=1, replica_groups=mesh['blk'=32,'team'=16] {'blk'}, dimensions={0} | all-to-all | bytes 786432 | tf_op jit(solution)/shard_map/all_to_all | solution.py:220
  44.7 7.7 %tile.1 = (bf16[3584,2048]{1,0:T(8,128)(2,1)}, bf16[512,2048]{1,0:T(8,128)(2,1)S(1)}, f32[16,32,128]{2,1,0:T(8,128)S(1)}) custom-call(f32[16,128]{1,0:T(8,128)S(1)} %get-tuple-element.19.inv_scale_ref, bf16[16,16,128]{2,1,0:T(8,128)(2,1)S(1)} %all_to_all.35.cols_ref, bf16[32,48,128]{2,1,0:T(8,128)(2,1)S(1)} %all_to_all.36.rows_ref), custom_call_target="tpu_custom_call" | custom-call | tf_op jit(solution)/shard_map/tile/pallas_call | solution.py:224
  52.4 12.1 %all_to_all.37.received_ref = f32[16,32,128]{2,1,0:T(8,128)S(1)} all-to-all(f32[16,32,128]{2,1,0:T(8,128)S(1)} %get-tuple-element.24), channel_id=1, replica_groups=mesh['blk'=32,'team'=16] {'team'}, dimensions={0} | all-to-all | bytes 524288 | tf_op jit(solution)/shard_map/all_to_all | solution.py:257
  64.5 0.9 combine.1
  65.4 21.4 %all_to_all.38.v_ref = bf16[32,64,128]{2,1,0:T(8,128)(2,1)S(1)} all-to-all(bf16[32,64,128]{2,1,0:T(8,128)(2,1)S(1)} %get-tuple-element.27), channel_id=1, replica_groups=mesh['blk'=32,'team'=16] {'blk'}, dimensions={0} | all-to-all | bytes 1048576 | tf_op jit(solution)/shard_map/all_to_all | solution.py:271
  86.8 6.6 %all-to-all-start.4 = ((bf16[16,64,128]{2,1,0:T(8,128)(2,1)}), bf16[16,64,128]{2,1,0:T(8,128)(2,1)S(1)}, u32[]{:S(2)}, u32[]{:S(2)}) async-start(bf16[16,64,128]{2,1,0:T(8,128)(2,1)} %get-tuple-element.28), calls=%async_computation.4 | async-start | bytes 524288 | tf_op jit(solution)/shard_map/all_to_all | solution.py:282
  93.3 5.8 %apply.1.partial_ref = f32[16,32,128]{2,1,0:T(8,128)S(1)} custom-call(bf16[3584,2048]{1,0:T(8,128)(2,1)} %get-tuple-element.22.tile_ref, bf16[512,2048]{1,0:T(8,128)(2,1)S(1)} %get-tuple-element.23.tail_ref, bf16[32,64,128]{2,1,0:T(8,128)(2,1)S(1)} %all_to_all.38.v_ref), custom_call_target="tpu_custom_call" | custom-call | flops 469762048 | bytes 14680064 | tf_op jit(solution)/shard_map/apply/pallas_call | solution.py:258
  99.1 1.4 %all-to-all-done.4.cols_ref = bf16[16,64,128]{2,1,0:T(8,128)(2,1)S(1)} async-done(((bf16[16,64,128]{2,1,0:T(8,128)(2,1)}), bf16[16,64,128]{2,1,0:T(8,128)(2,1)S(1)}, u32[]{:S(2)}, u32[]{:S(2)}) %all-to-all-start.4) | async-done | bytes 262176 | tf_op jit(solution)/shard_map/all_to_all | solution.py:282
  100.6 0.2 pack.1
  100.8 10.9 %all_to_all.39 = bf16[16,48,128]{2,1,0:T(8,128)(2,1)S(1)} all-to-all(bf16[16,48,128]{2,1,0:T(8,128)(2,1)S(1)} %get-tuple-element.32), channel_id=1, replica_groups=mesh['blk'=32,'team'=16] {'team'}, dimensions={0} | all-to-all | bytes 393216 | tf_op jit(solution)/shard_map/all_to_all | solution.py:283
  111.7 16.2 %all_to_all.40 = f32[32,2,128]{2,1,0:T(2,128)S(1)} all-to-all(f32[32,2,128]{2,1,0:T(2,128)S(1)} %broadcast_in_dim.18), channel_id=1, replica_groups=mesh['blk'=32,'team'=16] {'blk'}, dimensions={0} | all-to-all | bytes 65536 | tf_op jit(solution)/shard_map/all_to_all | solution.py:288
  127.9 0.1 broadcast_add_fusion
  128.0 0.1 fusion.9
  128.1 0.7 fusion.6
  (4 shorter events, 0.1 us)
Async XLA Ops:
  86.8 13.8 %all-to-all-start.4 = ((bf16[16,64,128]{2,1,0:T(8,128)(2,1)}), bf16[16,64,128]{2,1,0:T(8,128)(2,1)S(1)}, u32[]{:S(2)}, u32[]{:S(2)}) async-start(bf16[16,64,128]{2,1,0:T(8,128)(2,1)} %get-tuple-element.28), calls=%async_computation.4 | async-start | bytes 524288 | tf_op jit(solution)/shard_map/all_to_all | solution.py:282
